TPU v7x, 128 devices: a whole 4x4x4 slice. The times are simulated.
128 devices in a mesh: tiles: 64 (over z, y, x), grp: 2 (over core).
Axes of the slice: x: 4, y: 4, z: 4, core: 2. Of those that a mesh axis runs over, the one named last changes fastest.
Arguments:
- strips: bfloat16 [256, 256, 4096], P(('tiles', 'grp'))
- edge_colour: int32 [128, 2], P(('tiles', 'grp')), may hold values from 0 to 1, as said below
- patch_offsets: int32 [128, 2, 16, 2], P(('tiles', 'grp')), may hold values from 0 to 3968, as said below
- patch_live: int32 [128, 2], P(('tiles', 'grp')), may hold values from 4 to 16
- node_ids: int32 [128, 2, 16], P(('tiles', 'grp')), may hold values from 0 to 16383
Outputs:
- node_sums: float32 [2, 16384], P(None, ('tiles', 'grp'))
Inputs may be any that keep to these rules, and one draw needn't show every extreme that they name: `edge_colour`: for each device its 2 entries name different strips. `patch_offsets`: A device and the device it is paired with in a round have the same offsets in that round. Rows are at most 128.
All inputs are finite; a program needn't handle non-finite values.
Results may differ from a plain program's by a relative error of at most 0.0003.
Values may be sent and summed in bfloat16 or wider, within the bound.
No kernel may reach another device: no remote copies, remote signals or barrier semaphores. Data moves between devices by JAX's collectives and lax.ppermute only.
A program may use at most 64 MiB of HBM per device.

v0:
```python
import math

import jax
import jax.numpy as jnp
from jax import lax
from jax.sharding import PartitionSpec as P

PATCH = 128
NODE_DEV = 128


highest = lax.Precision.HIGHEST


def from_partner(x, axis, stride):
    return lax.ppermute(x, axis, [(i, i ^ 1 << stride) for i in range(lax.axis_size(axis))])


def tables(length):
    indices = jnp.arange(length, dtype=jnp.int32)
    product = indices[:, None] * indices[None, :] % length
    angles = product.astype(jnp.float32) * (2.0 * math.pi / length)
    return (jnp.cos(angles), jnp.sin(angles))


def right_mul(patches, matrix):
    return jnp.einsum("pab,bc->pac", patches, matrix, precision=highest)


def left_mul(matrix, patches):
    return jnp.einsum("ab,pbc->pac", matrix, patches, precision=highest)


def forward(patches, cosine, sine):
    real_half = right_mul(patches, cosine)
    imag_half = -right_mul(patches, sine)
    return (
        left_mul(cosine, real_half) + left_mul(sine, imag_half),
        left_mul(cosine, imag_half) - left_mul(sine, real_half),
    )


def displacement_parts(first_set, second_set):
    length = first_set.shape[-1]
    cosine, sine = tables(length)
    first_real, first_imag = forward(first_set, cosine, sine)
    second_real, second_imag = forward(second_set, cosine, sine)
    cross_real = first_real * second_real + first_imag * second_imag
    cross_imag = first_imag * second_real - first_real * second_imag
    magnitude = jnp.sqrt(cross_real * cross_real + cross_imag * cross_imag)
    denominator = magnitude + 0.1 * jnp.mean(magnitude, axis=(1, 2), keepdims=True) + 1e-06
    white_real = cross_real / denominator
    white_imag = cross_imag / denominator
    back_real = left_mul(cosine, white_real) - left_mul(sine, white_imag)
    back_imag = left_mul(cosine, white_imag) + left_mul(sine, white_real)
    surface = (right_mul(back_real, cosine) - right_mul(back_imag, sine)) / float(length * length)
    flattened = surface.reshape(surface.shape[0], length * length)
    centre = jnp.mean(flattened, axis=1, keepdims=True)
    spread = jnp.sqrt(
        jnp.mean((flattened - centre) * (flattened - centre), axis=1, keepdims=True) + 1e-06
    )
    scores = 2.0 * (flattened - centre) / spread
    weights = jax.nn.softmax(scores, axis=-1).reshape(surface.shape)
    coords = ((jnp.arange(length, dtype=jnp.int32) + length // 2) % length - length // 2).astype(
        jnp.float32
    )
    coord_scale = float(length // 8)
    row_shift = jnp.sum(weights * coords[None, :, None], axis=(1, 2)) / coord_scale
    col_shift = jnp.sum(weights * coords[None, None, :], axis=(1, 2)) / coord_scale
    row_edge = jnp.sum(weights[:, length // 2, :], axis=1)
    col_edge = jnp.sum(weights[:, :, length // 2], axis=1)
    return (jnp.stack([row_shift, col_shift]), jnp.stack([row_edge, col_edge]))


def window_stack(strip, offsets, length):

    def single(corner):
        return lax.dynamic_slice(strip, (corner[0], corner[1]), (length, length))

    return jax.vmap(single)(offsets)


def on_device(strips, edge_colour, patch_offsets, patch_live, node_ids):
    rounds = strips.shape[0]
    length = PATCH
    slot_count = patch_offsets.shape[2]
    tile_count = lax.axis_size("tiles")
    group_count = lax.axis_size("grp")
    first_list = []
    second_list = []
    for round_index in range(rounds):
        pair_bit = 0 if round_index == 0 else tile_count.bit_length() - 2
        own_strip = lax.dynamic_index_in_dim(strips, edge_colour[0, round_index], 0, keepdims=False)
        corners = patch_offsets[0, round_index]
        own_windows = window_stack(own_strip, corners, length)
        other_strip = from_partner(own_strip, "tiles", pair_bit)
        other_windows = window_stack(other_strip, corners, length)
        first_list.append(own_windows)
        second_list.append(other_windows)
    first_set = jnp.concatenate(first_list, axis=0).astype(jnp.float32)
    second_set = jnp.concatenate(second_list, axis=0).astype(jnp.float32)
    shifts, unused_edges = displacement_parts(first_set, second_set)
    slot_index = jnp.arange(slot_count, dtype=jnp.int32)
    live_mask = (slot_index[None, :] < patch_live[0][:, None]).reshape(rounds * slot_count)
    values = jnp.where(live_mask[None, :], shifts, jnp.zeros_like(shifts))
    node_list = node_ids[0].reshape(rounds * slot_count)
    total_nodes = NODE_DEV * tile_count * group_count
    onehot = (node_list[:, None] == jnp.arange(total_nodes, dtype=jnp.int32)[None, :]).astype(
        jnp.float32
    )
    term_table = jnp.dot(values, onehot, precision=highest, preferred_element_type=jnp.float32)
    return lax.psum_scatter(term_table, ("tiles", "grp"), scatter_dimension=1, tiled=True)


def solution(mesh):
    placed = (
        P(("tiles", "grp"), None, None),
        P(("tiles", "grp"), None),
        P(("tiles", "grp"), None, None, None),
        P(("tiles", "grp"), None),
        P(("tiles", "grp"), None, None),
    )
    return jax.shard_map(
        on_device, mesh=mesh, in_specs=placed, out_specs=P(None, ("tiles", "grp")), check_vma=False
    )
```

profile of v0, /device:TPU:0, one launch (start us, length us, event | category | flops | bytes accessed | tf_op | source)
XLA Modules:
  0.0 946.0 jit_solution(7362290066601205663)
XLA Ops:
  11.6 4.7 dynamic-slice_bitcast_fusion
  17.9 3.9 collective-permute-start.1
  21.9 47.5 %while.4 = (s32[]{:T(128)}, bf16[256,4096]{1,0:T(8,128)(2,1)}, s32[16,2]{0,1:T(2,128)S(1)}, bf16[16,128,128]{2,1,0:T(8,128)(2,1)S(1)}, s32[]{:T(128)}) while((s32[]{:T(128)}, bf16[256,4096]{1,0:T(8,128)(2,1)}, s32[16,2]{0,1:T(2,128)S(1)}, bf16[16,128,128]{2,1,0:T(8,128)(2,1)S(1)}, s32[]{:T(128)}) %tuple.79), condition=%wide.while_cond, body=%wide.while_body.sunk | while | flops 2 | bytes 65645 | solution.py:78
  25.4 2.3 bitcast_dynamic-update-slice_fusion.8
  28.4 2.3 bitcast_dynamic-update-slice_fusion.8
  31.4 2.3 bitcast_dynamic-update-slice_fusion.8
  34.3 2.3 bitcast_dynamic-update-slice_fusion.8
  37.3 2.3 bitcast_dynamic-update-slice_fusion.8
  40.3 2.3 bitcast_dynamic-update-slice_fusion.8
  43.3 2.3 bitcast_dynamic-update-slice_fusion.8
  46.2 2.3 bitcast_dynamic-update-slice_fusion.8
  49.2 2.3 bitcast_dynamic-update-slice_fusion.8
  52.2 2.3 bitcast_dynamic-update-slice_fusion.8
  55.2 2.3 bitcast_dynamic-update-slice_fusion.8
  58.1 2.3 bitcast_dynamic-update-slice_fusion.8
  61.1 2.3 bitcast_dynamic-update-slice_fusion.8
  64.1 2.3 bitcast_dynamic-update-slice_fusion.8
  67.1 2.3 bitcast_dynamic-update-slice_fusion.8
  69.5 47.3 %while.5 = (s32[]{:T(128)}, bf16[256,4096]{1,0:T(8,128)(2,1)}, s32[16,2]{0,1:T(2,128)S(1)}, bf16[16,128,128]{2,1,0:T(8,128)(2,1)S(1)}, s32[]{:T(128)}) while((s32[]{:T(128)}, bf16[256,4096]{1,0:T(8,128)(2,1)}, s32[16,2]{0,1:T(2,128)S(1)}, bf16[16,128,128]{2,1,0:T(8,128)(2,1)S(1)}, s32[]{:T(128)}) %tuple.82), condition=%wide.while_cond.1, body=%wide.while_body.1.sunk | while | flops 2 | bytes 65645 | solution.py:78
  73.0 2.3 bitcast_dynamic-update-slice_fusion.9
  76.0 2.3 bitcast_dynamic-update-slice_fusion.9
  79.0 2.3 bitcast_dynamic-update-slice_fusion.9
  81.9 2.3 bitcast_dynamic-update-slice_fusion.9
  84.9 2.3 bitcast_dynamic-update-slice_fusion.9
  87.9 2.3 bitcast_dynamic-update-slice_fusion.9
  90.8 2.3 bitcast_dynamic-update-slice_fusion.9
  93.8 2.3 bitcast_dynamic-update-slice_fusion.9
  96.8 2.3 bitcast_dynamic-update-slice_fusion.9
  99.7 2.3 bitcast_dynamic-update-slice_fusion.9
  102.7 2.3 bitcast_dynamic-update-slice_fusion.9
  105.6 2.3 bitcast_dynamic-update-slice_fusion.9
  108.6 2.3 bitcast_dynamic-update-slice_fusion.9
  111.6 2.3 bitcast_dynamic-update-slice_fusion.9
  114.5 2.3 bitcast_dynamic-update-slice_fusion.9
  121.9 3.4 fusion.44
  125.3 4.9 fusion.20
  130.3 46.8 %while.6 = (s32[]{:T(128)}, bf16[256,4096]{1,0:T(8,128)(2,1)}, s32[16,2]{0,1:T(2,128)S(1)}, bf16[16,128,128]{2,1,0:T(8,128)(2,1)S(1)}, s32[]{:T(128)}) while((s32[]{:T(128)}, bf16[256,4096]{1,0:T(8,128)(2,1)}, s32[16,2]{0,1:T(2,128)S(1)}, bf16[16,128,128]{2,1,0:T(8,128)(2,1)S(1)}, s32[]{:T(128)}) %tuple.88), condition=%wide.while_cond.2, body=%wide.while_body.2.sunk | while | flops 2 | bytes 65645 | solution.py:78
  136.8 2.2 bitcast_dynamic-update-slice_fusion.10
  179.9 57.6 %while.7 = (s32[]{:T(128)}, bf16[256,4096]{1,0:T(8,128)(2,1)}, s32[16,2]{0,1:T(2,128)S(1)}, bf16[16,128,128]{2,1,0:T(8,128)(2,1)}, s32[]{:T(128)}) while((s32[]{:T(128)}, bf16[256,4096]{1,0:T(8,128)(2,1)}, s32[16,2]{0,1:T(2,128)S(1)}, bf16[16,128,128]{2,1,0:T(8,128)(2,1)}, s32[]{:T(128)}) %tuple.87), condition=%wide.while_cond.3, body=%wide.while_body.3.sunk | while | flops 2 | bytes 67169 | solution.py:78
  180.6 2.8 bitcast_dynamic-update-slice_fusion.11
  184.1 2.9 bitcast_dynamic-update-slice_fusion.11
  187.7 2.9 bitcast_dynamic-update-slice_fusion.11
  191.2 2.9 bitcast_dynamic-update-slice_fusion.11
  194.8 2.9 bitcast_dynamic-update-slice_fusion.11
  198.4 2.9 bitcast_dynamic-update-slice_fusion.11
  202.0 2.9 bitcast_dynamic-update-slice_fusion.11
  205.6 2.9 bitcast_dynamic-update-slice_fusion.11
  209.2 2.9 bitcast_dynamic-update-slice_fusion.11
  212.8 2.9 bitcast_dynamic-update-slice_fusion.11
  216.4 2.9 bitcast_dynamic-update-slice_fusion.11
  220.0 2.9 bitcast_dynamic-update-slice_fusion.11
  223.6 2.9 bitcast_dynamic-update-slice_fusion.11
  227.1 2.9 bitcast_dynamic-update-slice_fusion.11
  230.7 2.9 bitcast_dynamic-update-slice_fusion.11
  234.3 2.9 bitcast_dynamic-update-slice_fusion.11
  245.5 3.7 fusion.26
  249.3 3.9 fusion.29
  253.2 5.0 fusion.32
  258.2 3.2 fusion.40
  261.5 3.5 fusion.55
  264.9 3.2 fusion.38
  268.2 3.2 fusion.52
  278.5 9.0 convolution_bitcast_fusion
  287.6 649.7 %reduce-scatter.4.cloned.1.call-done = f32[128,2]{1,0:T(8,128)} async-done(((f32[16384,2]{1,0:T(8,128)}), f32[128,2]{1,0:T(8,128)}) %reduce-scatter.4.cloned.1.call-update) | async-done | bytes 1040
  (198 shorter events, 108.0 us)
Async XLA Ops:
  6.5 930.7 %reduce-scatter.4.cloned.1.call-start = ((), (), s32[]{:S(2)}) async-start(), calls=%async_computation.1 | async-start | bytes 8454144
  11.6 10.2 %copy-start.3 = (s32[1,2,16,2]{2,3,1,0:T(2,128)S(1)}, s32[1,2,16,2]{2,3,1,0:T(2,128)}, u32[]{:S(2)}) copy-start(s32[1,2,16,2]{2,3,1,0:T(2,128)} %param.7) | copy-start | bytes 772
  11.6 105.3 %copy-start.5 = (s32[1,2]{1,0:T(1,128)S(1)}, s32[1,2]{1,0:T(1,128)}, u32[]{:S(2)}) copy-start(s32[1,2]{1,0:T(1,128)} %param.8) | copy-start | bytes 28
  16.3 100.7 %copy-start.4 = (s32[1,2,16]{2,1,0:T(2,128)S(1)}, s32[1,2,16]{2,1,0:T(2,128)}, u32[]{:S(2)}) copy-start(s32[1,2,16]{2,1,0:T(2,128)} %param.9) | copy-start | bytes 388
  16.3 114.0 %collective-permute-start = (bf16[256,4096]{1,0:T(8,128)(2,1)}, bf16[256,4096]{1,0:T(8,128)(2,1)}, u32[]{:S(2)}, u32[]{:S(2)}) collective-permute-start(bf16[256,4096]{1,0:T(8,128)(2,1)} %get-tuple-element.245), channel_id=1, source_target_pairs={{0,2},{2,0},{4,6},{6,4},{8,10},{10,8},{12,14},{14,12},{16,18},{18,... | collective-permute-start | bytes 6291464 | tf_op jit(solution)/shard_map/ppermute | solution.py:16
  17.9 161.2 %collective-permute-start.1 = (bf16[256,4096]{1,0:T(8,128)(2,1)}, bf16[256,4096]{1,0:T(8,128)(2,1)}, u32[]{:S(2)}, u32[]{:S(2)}) collective-permute-start(bf16[256,4096]{1,0:T(8,128)(2,1)} %get-tuple-element.260), channel_id=1, source_target_pairs={{0,64},{2,66},{4,68},{6,70},{8,72},{10,74},{12,76},{14,78},{16,80}... | collective-permute-start | bytes 6291464 | tf_op jit(solution)/shard_map/ppermute | solution.py:16
  177.1 0.8 copy-start.2
  249.3 3.9 copy-start
  249.3 3.9 copy-start.1
Sparse Core Ops, SparseCore 0:
  287.7 649.5 reduce-scatter.3
where the time goes:
time: 959 us; the launch traced here: 946 us
  waiting for transfers between devices  650 us (68%)
  local copies, waits for them, and re-layouts  210 us (22%)
  matrix products  58.9 us (6%)
  between operations  17.8 us (2%)
    unnamed x2, waiting for transfers between devices  650 us
    gather x192, local copies, waits for them, and re-layouts  198 us
    dot_general x12, matrix products, left_mul(): return jnp.einsum('ab,pbc->pac', matrix, patches, precision=highest)  40.5 us
  transfers between devices with their start and end apart: 3, of which 1 were waited for; matrix products, arithmetic and copies ran while one was open for 16% of the time, Pallas kernels for 0%

commit v1 on v0

v1 whole, which is shorter than its diff:
```python
import functools
import math

import jax
import jax.numpy as jnp
import ml_dtypes
import numpy as np
from jax import lax
from jax.experimental import pallas as pl
from jax.experimental.pallas import tpu as pltpu
from jax.sharding import PartitionSpec as P

SIDE = 128
HALF = 8
SLOTS = 16
CELLS = SIDE * SIDE
BITS = (0, 5)

f32 = jnp.float32
bf16 = jnp.bfloat16


def fourier_tables():
    index = np.arange(SIDE)
    angle = (np.outer(index, index) % SIDE) * (2.0 * math.pi / SIDE)
    cosine, sine = np.cos(angle), np.sin(angle)

    def pieces(table):
        high = table.astype(ml_dtypes.bfloat16)
        low = (table - high.astype(np.float64)).astype(ml_dtypes.bfloat16)
        return high, low

    cos_high, cos_low = pieces(cosine)
    sin_high, sin_low = pieces(sine)
    first = np.block([[cos_high, sin_high], [cos_low, sin_low]])
    left_high = np.block([[cos_high, -sin_high], [sin_high, cos_high]])
    left_low = np.block([[cos_low, -sin_low], [sin_low, cos_low]])
    left = np.concatenate([left_high, left_low, left_high], axis=1)
    right = np.concatenate([left_high.T, left_high.T, left_low.T], axis=0)
    return first, left, right


def tile_side(bit):
    return (lax.axis_index("tiles") >> bit) & 1


def cut_kernel(rounds, mine, colour_ref, corner_ref, strips_ref, out_ref, blocks, sems):
    rows = lax.broadcasted_iota(jnp.int32, (SIDE, 2 * SIDE), 0)
    lanes = lax.broadcasted_iota(jnp.int32, (SIDE, SIDE), 1)
    last = strips_ref.shape[2] // SIDE - 2
    plan = []
    for round_index in rounds:
        side = tile_side(BITS[round_index])
        start = HALF * side if mine else HALF - HALF * side
        for j in range(HALF):
            place = (round_index * SLOTS + start + j) * 2
            row = corner_ref[place]
            col = corner_ref[place + 1]
            block = jnp.minimum(col >> 7, last)
            source = strips_ref.at[
                colour_ref[round_index], :, pl.ds(pl.multiple_of(block * SIDE, SIDE), 2 * SIDE)
            ]
            copy = pltpu.make_async_copy(source, blocks.at[len(plan)], sems.at[len(plan)])
            copy.start()
            plan.append((copy, row, col - block * SIDE))
    for i, (copy, row, shift) in enumerate(plan):
        copy.wait()
        top = blocks[i, :SIDE, :].astype(f32)
        bottom = blocks[i, SIDE:, :].astype(f32)
        both = jnp.where(rows >= row, top, bottom)
        window = jnp.where(lanes >= shift, both[:, :SIDE], both[:, SIDE:])
        out_ref[i] = window.astype(bf16)


def cut(rounds, mine, colour, corners, strips):
    count = len(rounds) * HALF
    return pl.pallas_call(
        functools.partial(cut_kernel, rounds, mine),
        out_shape=jax.ShapeDtypeStruct((count, SIDE, SIDE), bf16),
        in_specs=[
            pl.BlockSpec(memory_space=pltpu.SMEM),
            pl.BlockSpec(memory_space=pltpu.SMEM),
            pl.BlockSpec(memory_space=pl.ANY),
        ],
        out_specs=pl.BlockSpec(memory_space=pltpu.VMEM),
        scratch_shapes=[
            pltpu.VMEM((count, 2 * SIDE, 2 * SIDE), bf16),
            pltpu.SemaphoreType.DMA((count,)),
        ],
        compiler_params=pltpu.CompilerParams(vmem_limit_bytes=24 * 1024 * 1024),
        cost_estimate=pl.CostEstimate(
            flops=count * CELLS * 8, bytes_accessed=count * CELLS * 10, transcendentals=0
        ),
    )(colour, corners, strips)


def split(x):
    high = x.astype(bf16)
    return high, (x - high.astype(f32)).astype(bf16)


def matmul(a, b):
    return jnp.dot(a, b, preferred_element_type=f32)


def left_mul(table, x):
    high, low = split(x)
    return matmul(table, jnp.concatenate([high, high, low], axis=0))


def right_mul(x, table):
    high, low = split(x)
    return matmul(jnp.concatenate([high, low, high], axis=1), table)


def forward_pair(first_window, second_window, first, left):
    parts = []
    for window in (first_window, second_window):
        parts.append(matmul(jnp.concatenate([window, window], axis=1), first))
    a, b = parts
    stacked = jnp.concatenate(
        [
            jnp.concatenate([a[:, :SIDE], b[:, :SIDE]], axis=1),
            jnp.concatenate([a[:, SIDE:], b[:, SIDE:]], axis=1),
        ],
        axis=0,
    )
    return left_mul(left, stacked)


def forward_kernel(window_ref, first_ref, left_ref, out_ref):
    for q in range(2):
        out_ref[q] = forward_pair(
            window_ref[2 * q], window_ref[2 * q + 1], first_ref[...], left_ref[...]
        )


def forward(windows, first, left):
    count = windows.shape[0]
    whole = lambda table: pl.BlockSpec(table.shape, lambda i: (0, 0))
    return pl.pallas_call(
        forward_kernel,
        grid=(count // 4,),
        out_shape=jax.ShapeDtypeStruct((count // 2, 2 * SIDE, 2 * SIDE), f32),
        in_specs=[
            pl.BlockSpec((4, SIDE, SIDE), lambda i: (i, 0, 0)),
            whole(first),
            whole(left),
        ],
        out_specs=pl.BlockSpec((2, 2 * SIDE, 2 * SIDE), lambda i: (i, 0, 0)),
        cost_estimate=pl.CostEstimate(
            flops=count * 8 * 2 * SIDE**3 * 2, bytes_accessed=count * CELLS * 10, transcendentals=0
        ),
    )(windows, first, left)


def total(x):
    return jnp.sum(jnp.sum(x, axis=0, keepdims=True), axis=1, keepdims=True)


def correlate_kernel(
    ids_ref, near_ref, window_ref, first_ref, left_ref, right_ref, out_ref, plain, ramp, edge
):
    step = pl.program_id(0)
    spectra = []
    for q in range(2):
        near = near_ref[q]
        far = forward_pair(
            window_ref[2 * q], window_ref[2 * q + 1], first_ref[...], left_ref[...]
        )
        near_real, near_imag = near[:SIDE], near[SIDE:]
        far_real, far_imag = far[:SIDE], far[SIDE:]
        cross_real = near_real * far_real + near_imag * far_imag
        cross_imag = near_real * far_imag - near_imag * far_real
        square = cross_real * cross_real + cross_imag * cross_imag
        magnitude = jnp.sqrt(square)
        whites = []
        for h in range(2):
            part = slice(h * SIDE, (h + 1) * SIDE)
            size = magnitude[:, part]
            scale = 1.0 / (size + (total(size) * (0.1 / CELLS) + 1e-6))
            whites.append((cross_real[:, part] * scale, cross_imag[:, part] * scale))
        (a_real, a_imag), (b_real, b_imag) = whites
        spectra.append((a_real - b_imag, a_imag + b_real))
    stacked = jnp.concatenate(
        [
            jnp.concatenate([spectra[0][0], spectra[1][0]], axis=1),
            jnp.concatenate([spectra[0][1], spectra[1][1]], axis=1),
        ],
        axis=0,
    )
    back = left_mul(left_ref[...], stacked)
    rows = jnp.concatenate(
        [
            jnp.concatenate([back[:SIDE, :SIDE], back[SIDE:, :SIDE]], axis=1),
            jnp.concatenate([back[:SIDE, SIDE:], back[SIDE:, SIDE:]], axis=1),
        ],
        axis=0,
    )
    surfaces = right_mul(rows, right_ref[...])
    row_index = lax.broadcasted_iota(jnp.int32, (SIDE, SIDE), 0)
    row_coord = (((row_index + SIDE // 2) & (SIDE - 1)) - SIDE // 2).astype(f32)
    for p in range(4):
        q, h = divmod(p, 2)
        surface = surfaces[q * SIDE : (q + 1) * SIDE, h * SIDE : (h + 1) * SIDE]
        mean = total(surface) * (1.0 / CELLS)
        variance = total(surface * surface) * (1.0 / CELLS) - mean * mean
        peak = jnp.max(jnp.max(surface, axis=0, keepdims=True), axis=1, keepdims=True)
        spread = jnp.sqrt(jnp.maximum(variance, 0.0) * (1.0 / CELLS**2) + 1e-6)
        factor = (2.0 / CELLS) / spread
        weight = jnp.exp((surface - peak) * factor)
        place = pl.ds(step * 4 + p, 1)
        plain[place, :] = jnp.sum(weight, axis=0, keepdims=True)
        ramp[place, :] = jnp.sum(weight * row_coord, axis=0, keepdims=True)
        edge[place, :] = weight[SIDE // 2 : SIDE // 2 + 1, :]

    @pl.when(step == pl.num_programs(0) - 1)
    def finish():
        lane = lax.broadcasted_iota(jnp.int32, (8, SIDE), 1)
        sublane = lax.broadcasted_iota(jnp.int32, (8, SIDE), 0)
        coord = (((lane + SIDE // 2) & (SIDE - 1)) - SIDE // 2).astype(f32)
        chosen = jnp.where(lane == SIDE // 2, 1.0, 0.0)
        query = jnp.where(sublane == 0, 1.0, jnp.where(sublane == 1, coord, chosen))

        def reduce(ref):
            return lax.dot_general(
                query,
                ref[...],
                (((1,), (1,)), ((), ())),
                precision=lax.Precision.HIGHEST,
                preferred_element_type=f32,
            )

        plain_sums, ramp_sums, edge_sums = reduce(plain), reduce(ramp), reduce(edge)
        inverse = 1.0 / plain_sums[0:1]
        scale = 8.0 / SIDE
        row_shift = ramp_sums[0:1] * inverse * scale
        col_shift = plain_sums[1:2] * inverse * scale
        row_other = -row_shift - edge_sums[0:1] * inverse * (SIDE * scale)
        col_other = -col_shift - plain_sums[2:3] * inverse * (SIDE * scale)
        out = ids_ref[...]
        lane = lax.broadcasted_iota(jnp.int32, (1, SIDE), 1)
        for i, value in enumerate((row_shift, col_shift, row_other, col_other)):
            moved = jnp.concatenate(
                [jnp.zeros((1, 32 + 16 * i), f32), value, jnp.zeros((1, 80 - 16 * i), f32)], axis=1
            )
            inside = (lane >= 32 + 16 * i) & (lane < 48 + 16 * i)
            out = jnp.where(inside, moved, out)
        out_ref[...] = out


def correlate(ids, near, windows, first, left, right):
    count = windows.shape[0]
    whole = lambda table: pl.BlockSpec(table.shape, lambda i: (0, 0))
    return pl.pallas_call(
        correlate_kernel,
        grid=(count // 4,),
        out_shape=jax.ShapeDtypeStruct((1, SIDE), f32),
        in_specs=[
            whole(ids),
            pl.BlockSpec((2, 2 * SIDE, 2 * SIDE), lambda i: (i, 0, 0)),
            pl.BlockSpec((4, SIDE, SIDE), lambda i: (i, 0, 0)),
            whole(first),
            whole(left),
            whole(right),
        ],
        out_specs=pl.BlockSpec((1, SIDE), lambda i: (0, 0)),
        scratch_shapes=[pltpu.VMEM((count, SIDE), f32)] * 3,
        cost_estimate=pl.CostEstimate(
            flops=count * 12 * 2 * SIDE**3 * 2,
            bytes_accessed=count * CELLS * 10,
            transcendentals=count * CELLS * 3,
        ),
    )(ids, near, windows, first, left, right)


def collect_kernel(packed_ref, out_ref):
    packed = packed_ref[...].T
    base = (lax.axis_index("tiles") * lax.axis_size("grp") + lax.axis_index("grp")) * SIDE
    device = lax.broadcasted_iota(jnp.int32, (HALF, SIDE), 1)
    node = lax.broadcasted_iota(jnp.int32, (SIDE, SIDE), 0).astype(f32)
    sums = [jnp.zeros((SIDE, SIDE), f32), jnp.zeros((SIDE, SIDE), f32)]
    for r, bit in enumerate(BITS):
        reach = 2 << bit
        side = (device >> (bit + 1)) & 1
        own, other = [], []
        for c in range(2):
            own.append(packed[32 + 16 * c + HALF * r :][:HALF])
            far = packed[64 + 16 * c + HALF * r :][:HALF]
            up = pltpu.roll(far, SIDE - reach, 1)
            down = pltpu.roll(far, reach, 1)
            other.append(jnp.where(side == 0, up, down))
        for h in range(2):
            local = packed[SLOTS * r + HALF * h :][:HALF] - base.astype(f32)
            values = [jnp.where(side == h, own[c], other[c]) for c in range(2)]
            for j in range(HALF):
                hit = node == local[j : j + 1]
                for c in range(2):
                    sums[c] = sums[c] + jnp.where(hit, values[c][j : j + 1], 0.0)
    ones = jnp.ones((8, SIDE), f32)
    for c in range(2):
        summed = lax.dot_general(
            ones,
            sums[c],
            (((1,), (1,)), ((), ())),
            precision=lax.Precision.HIGHEST,
            preferred_element_type=f32,
        )
        out_ref[c : c + 1] = summed[0:1]


def collect(packed):
    return pl.pallas_call(
        collect_kernel,
        out_shape=jax.ShapeDtypeStruct((2, SIDE), f32),
        in_specs=[pl.BlockSpec(memory_space=pltpu.VMEM)],
        out_specs=pl.BlockSpec(memory_space=pltpu.VMEM),
    )(packed)


def swap(x, bit):
    pairs = [(i, i ^ (1 << bit)) for i in range(lax.axis_size("tiles"))]
    return lax.ppermute(x, "tiles", pairs)


def on_device(strips, edge_colour, patch_offsets, patch_live, node_ids):
    first, left, right = (jnp.asarray(table) for table in fourier_tables())
    colour = edge_colour.reshape(2)
    corners = patch_offsets.reshape(4 * SLOTS)
    far_late = swap(cut((1,), False, colour, corners, strips), BITS[1])
    far_early = swap(cut((0,), False, colour, corners, strips), BITS[0])
    near = forward(cut((0, 1), True, colour, corners, strips), first, left)
    slot = jnp.arange(SLOTS, dtype=jnp.int32)
    live = slot[None, :] < patch_live[0][:, None]
    ids = jnp.where(live, node_ids[0], -1).astype(f32).reshape(1, 2 * SLOTS)
    ids = jnp.pad(ids, ((0, 0), (0, SIDE - 2 * SLOTS)))
    far = jnp.concatenate([far_early, far_late], axis=0)
    packed = correlate(ids, near, far, first, left, right)
    spread = jnp.broadcast_to(packed, (SIDE, SIDE))
    gathered = lax.all_to_all(spread, ("tiles", "grp"), 0, 0, tiled=True)
    return collect(gathered)


def solution(mesh):
    placed = (
        P(("tiles", "grp"), None, None),
        P(("tiles", "grp"), None),
        P(("tiles", "grp"), None, None, None),
        P(("tiles", "grp"), None),
        P(("tiles", "grp"), None, None),
    )
    return jax.shard_map(
        on_device, mesh=mesh, in_specs=placed, out_specs=P(None, ("tiles", "grp")), check_vma=False
    )
```

time: 959 us -> 52.2 us (0.05)
  the two profiles are of different devices: /device:TPU:0 before, /device:TPU:1 now
where the time goes in v1:
time: 52.2 us; the launch traced here: 51.9 us
  Pallas kernels  19.3 us (37%)
  blocking collectives  17.7 us (34%)
  local copies, waits for them, and re-layouts  8.04 us (15%)
  starting transfers between devices  5.8 us (11%)
  other arithmetic  0.94 us (2%)
    all_to_all x1, blocking collectives, on_device(): gathered = lax.all_to_all(spread, ('tiles', 'grp'), 0, 0, tiled=True)  17.7 us
    pallas_call x1, Pallas kernels, correlate(): pl.pallas_call(correlate_kernel, grid=(count // 4,), out_shape=jax.ShapeD...  8.69 us
    unnamed x15, local copies, waits for them, and re-layouts  6.61 us
    ppermute x2, starting transfers between devices, swap(): return lax.ppermute(x, 'tiles', pairs)  5.8 us
    pallas_call x1, Pallas kernels, forward(): pl.pallas_call(forward_kernel, grid=(count // 4,), out_shape=jax.ShapeDty...  4.82 us
    pallas_call x3, Pallas kernels, cut(): pl.pallas_call(functools.partial(cut_kernel, rounds, mine), out_shape=jax...  3.53 us
    pallas_call x1, Pallas kernels, collect(): pl.pallas_call(collect_kernel, out_shape=jax.ShapeDtypeStruct((2, SIDE),...  2.27 us
  transfers between devices with their start and end apart: 2, of which 0 were waited for; matrix products, arithmetic and copies ran while one was open for 1% of the time, Pallas kernels for 14%

profile of v1, /device:TPU:1, one launch (start us, length us, event | category | flops | bytes accessed | tf_op | source)
XLA Modules:
  0.0 51.9 jit_solution(12151928592809318544)
XLA Ops:
  0.0 0.8 %copy.11 = s32[1,2,16,2]{3,2,1,0:T(8,128)S(1)} copy(s32[1,2,16,2]{2,3,1,0:T(2,128)} %param.10) | data formatting | bytes 512 | tf_op args[2]
  0.8 0.1 reshape.50.corner_ref
  0.9 0.0 copy-start
  0.9 2.2 %copy-done = bf16[2,256,4096]{2,1,0:T(8,128)(2,1)S(1)} copy-done((bf16[2,256,4096]{2,1,0:T(8,128)(2,1)S(1)}, bf16[2,256,4096]{2,1,0:T(8,128)(2,1)}, u32[]{:S(2)}) %copy-start) | copy-done | bytes 4194328
  3.1 0.0 copy-start.3
  3.1 0.7 %copy-done.3 = s32[1,2]{1,0:T(1,128)S(1)} copy-done((s32[1,2]{1,0:T(1,128)S(1)}, s32[1,2]{1,0:T(1,128)}, u32[]{:S(2)}) %copy-start.3) | copy-done | bytes 32
  3.7 0.0 copy-start.6
  3.7 0.0 copy-start.5
  3.7 0.0 copy-start.4
  3.7 1.0 %shard_map.84 = bf16[8,128,128]{2,1,0:T(8,128)(2,1)S(1)} custom-call(s32[2]{0:T(128)S(1)} %bitcast.6, s32[64]{0:T(128)S(1)} %reshape.50.corner_ref, bf16[2,256,4096]{2,1,0:T(8,128)(2,1)S(1)} %copy-done), custom_call_target="tpu_custom_call" | custom-call | flops 1048576 | bytes 1310720 | tf_op jit(solution)/shard_map/pallas_call | solution.py:77
  4.8 2.1 %collective-permute-start = (bf16[8,128,128]{2,1,0:T(8,128)(2,1)S(1)}, bf16[8,128,128]{2,1,0:T(8,128)(2,1)S(1)}, u32[]{:S(2)}, u32[]{:S(2)}) collective-permute-start(bf16[8,128,128]{2,1,0:T(8,128)(2,1)S(1)} %shard_map.84), channel_id=1, source_target_pairs={{0,2},{2,0},{4,6},{6,4},{8,10},{10,8},{12,14},{14,12},{16,18},{18,... | collective-permute-start | bytes 786440 | tf_op jit(solution)/shard_map/ppermute | solution.py:323
  6.9 1.0 %shard_map.85 = bf16[8,128,128]{2,1,0:T(8,128)(2,1)S(1)} custom-call(s32[2]{0:T(128)S(1)} %bitcast.7, s32[64]{0:T(128)S(1)} %reshape.50.corner_ref, bf16[2,256,4096]{2,1,0:T(8,128)(2,1)S(1)} %copy-done), custom_call_target="tpu_custom_call" | custom-call | flops 1048576 | bytes 1310720 | tf_op jit(solution)/shard_map/pallas_call | solution.py:77
  7.9 3.7 %collective-permute-start.1 = (bf16[8,128,128]{2,1,0:T(8,128)(2,1)S(1)}, bf16[8,128,128]{2,1,0:T(8,128)(2,1)S(1)}, u32[]{:S(2)}, u32[]{:S(2)}) collective-permute-start(bf16[8,128,128]{2,1,0:T(8,128)(2,1)S(1)} %shard_map.85), channel_id=1, source_target_pairs={{0,64},{2,66},{4,68},{6,70},{8,72},{10,74},{12,76},{14,78},{16,80}... | collective-permute-start | bytes 786440 | tf_op jit(solution)/shard_map/ppermute | solution.py:323
  11.6 0.0 copy-done.6
  11.6 0.1 iota_compare_fusion
  11.7 0.1 lt.29
  11.7 0.0 copy-done.5
  11.7 0.1 squeeze.3
  11.8 0.5 pad.4.ids_ref
  12.4 0.0 copy-done.4
  12.4 0.0 copy-start.1
  12.4 2.2 %copy-done.1 = bf16[2,256,4096]{2,1,0:T(8,128)(2,1)S(1)} copy-done((bf16[2,256,4096]{2,1,0:T(8,128)(2,1)S(1)}, bf16[2,256,4096]{2,1,0:T(8,128)(2,1)}, u32[]{:S(2)}) %copy-start.1) | copy-done | bytes 4194328
  14.5 1.5 %shard_map.82.window_ref = bf16[16,128,128]{2,1,0:T(8,128)(2,1)S(1)} custom-call(s32[2]{0:T(128)S(1)} %bitcast.8, s32[64]{0:T(128)S(1)} %reshape.50.corner_ref, bf16[2,256,4096]{2,1,0:T(8,128)(2,1)S(1)} %copy-done.1), custom_call_target="tpu_custom_call" | custom-call | flops 2097152 | bytes 2621440 | tf_op jit(solution)/shard_map/pallas_call | solution.py:77
  16.0 0.0 copy-start.2
  16.0 0.8 %copy-done.2 = bf16[16,128,128]{2,1,0:T(8,128)(2,1)} copy-done((bf16[16,128,128]{2,1,0:T(8,128)(2,1)}, bf16[16,128,128]{2,1,0:T(8,128)(2,1)S(1)}, u32[]{:S(2)}) %copy-start.2) | copy-done | bytes 524312
  16.9 4.8 %shard_map.83.near_ref = f32[8,256,256]{2,1,0:T(8,128)} custom-call(bf16[16,128,128]{2,1,0:T(8,128)(2,1)} %copy-done.2, bf16[256,256]{1,0:T(8,128)(2,1)} %constant.11.clone.first_ref, bf16[256,768]{1,0:T(8,128)(2,1)} %constant.12.clone.left_ref), custom_call_target="tpu_custom_call" | custom-call | flops 1073741824 | bytes 2621440 | tf_op jit(solution)/shard_map/pallas_call | solution.py:141
  21.7 0.0 collective-permute-done
  21.7 0.0 collective-permute-done.1
  21.7 0.9 %pad_maximum_fusion.window_ref = bf16[16,128,128]{2,1,0:T(8,128)(2,1)} fusion(bf16[8,128,128]{2,1,0:T(8,128)(2,1)S(1)} %collective-permute-done.1, bf16[8,128,128]{2,1,0:T(8,128)(2,1)S(1)} %collective-permute-done), kind=kLoop, calls=%fused_computation | loop fusion | flops 262144 | bytes 1048576 | tf_op jit(solution)/shard_map/concatenate | solution.py:337
  22.5 8.7 %shard_map.86 = f32[1,128]{1,0:T(1,128)} custom-call(f32[1,128]{1,0:T(1,128)} %pad.4.ids_ref, f32[8,256,256]{2,1,0:T(8,128)} %shard_map.83.near_ref, bf16[16,128,128]{2,1,0:T(8,128)(2,1)} %pad_maximum_fusion.window_ref, bf16[256,256]{1,0:T(8,128)(2,1)} %constant.11.clone.first_ref, bf16[256,768]{1,0:T(8,128)(2,1)} %constant.12.clone.left_ref, ...), custom_call_target="tpu_custom_call" | custom-call | flops 1610612736 | bytes 2621440 | tf_op jit(solution)/shard_map/pallas_call | solution.py:255
  31.2 0.6 %broadcast_in_dim.11 = f32[128,1,128]{2,1,0:T(1,128)S(1)} broadcast(f32[128]{0:T(128)} %bitcast.10), dimensions={2} | broadcast | bytes 66048 | tf_op jit(solution)/shard_map/broadcast_in_dim | solution.py:339
  31.9 17.7 %all_to_all.8 = f32[128,1,128]{2,1,0:T(1,128)} all-to-all(f32[128,1,128]{2,1,0:T(1,128)S(1)} %broadcast_in_dim.11), channel_id=1, replica_groups=mesh['tiles'=64,'grp'=2] {'tiles','grp'}, dimensions={0} | all-to-all | bytes 131072 | tf_op jit(solution)/shard_map/all_to_all | solution.py:340
  49.6 2.3 %shard_map.87 = f32[2,128]{1,0:T(2,128)} custom-call(f32[128,128]{1,0:T(8,128)} %bitcast.9), custom_call_target="tpu_custom_call" | custom-call | tf_op jit(solution)/shard_map/pallas_call | solution.py:313
  (1 shorter events, 0.0 us)
Async XLA Ops:
  0.9 2.2 %copy-start = (bf16[2,256,4096]{2,1,0:T(8,128)(2,1)S(1)}, bf16[2,256,4096]{2,1,0:T(8,128)(2,1)}, u32[]{:S(2)}) copy-start(bf16[2,256,4096]{2,1,0:T(8,128)(2,1)} %strips_ref.5) | copy-start | bytes 12582916
  3.1 0.7 %copy-start.3 = (s32[1,2]{1,0:T(1,128)S(1)}, s32[1,2]{1,0:T(1,128)}, u32[]{:S(2)}) copy-start(s32[1,2]{1,0:T(1,128)} %param.9) | copy-start | bytes 28
  3.7 7.9 %copy-start.6 = (s32[1,2]{1,0:T(1,128)S(1)}, s32[1,2]{1,0:T(1,128)}, u32[]{:S(2)}) copy-start(s32[1,2]{1,0:T(1,128)} %param.11) | copy-start | bytes 28
  3.7 8.0 %copy-start.5 = (s32[1,2,16]{2,1,0:T(2,128)S(1)}, s32[1,2,16]{2,1,0:T(2,128)}, u32[]{:S(2)}) copy-start(s32[1,2,16]{2,1,0:T(2,128)} %param.12) | copy-start | bytes 388
  3.7 8.6 %copy-start.4 = (s32[1,2]{1,0:T(1,128)S(1)}, s32[1,2]{1,0:T(1,128)}, u32[]{:S(2)}) copy-start(s32[1,2]{1,0:T(1,128)} %param.9) | copy-start | bytes 28
  4.8 16.9 %collective-permute-start = (bf16[8,128,128]{2,1,0:T(8,128)(2,1)S(1)}, bf16[8,128,128]{2,1,0:T(8,128)(2,1)S(1)}, u32[]{:S(2)}, u32[]{:S(2)}) collective-permute-start(bf16[8,128,128]{2,1,0:T(8,128)(2,1)S(1)} %shard_map.84), channel_id=1, source_target_pairs={{0,2},{2,0},{4,6},{6,4},{8,10},{10,8},{12,14},{14,12},{16,18},{18,... | collective-permute-start | bytes 786440 | tf_op jit(solution)/shard_map/ppermute | solution.py:323
  7.9 13.8 %collective-permute-start.1 = (bf16[8,128,128]{2,1,0:T(8,128)(2,1)S(1)}, bf16[8,128,128]{2,1,0:T(8,128)(2,1)S(1)}, u32[]{:S(2)}, u32[]{:S(2)}) collective-permute-start(bf16[8,128,128]{2,1,0:T(8,128)(2,1)S(1)} %shard_map.85), channel_id=1, source_target_pairs={{0,64},{2,66},{4,68},{6,70},{8,72},{10,74},{12,76},{14,78},{16,80}... | collective-permute-start | bytes 786440 | tf_op jit(solution)/shard_map/ppermute | solution.py:323
  12.4 2.2 %copy-start.1 = (bf16[2,256,4096]{2,1,0:T(8,128)(2,1)S(1)}, bf16[2,256,4096]{2,1,0:T(8,128)(2,1)}, u32[]{:S(2)}) copy-start(bf16[2,256,4096]{2,1,0:T(8,128)(2,1)} %strips_ref.5) | copy-start | bytes 12582916
  16.0 0.8 %copy-start.2 = (bf16[16,128,128]{2,1,0:T(8,128)(2,1)}, bf16[16,128,128]{2,1,0:T(8,128)(2,1)S(1)}, u32[]{:S(2)}) copy-start(bf16[16,128,128]{2,1,0:T(8,128)(2,1)S(1)} %shard_map.82.window_ref) | copy-start | bytes 1572868

commit v2 on v1

v2 whole, which is shorter than its diff:
```python
import functools
import math

import jax
import jax.numpy as jnp
import ml_dtypes
import numpy as np
from jax import lax
from jax.experimental import pallas as pl
from jax.experimental.pallas import tpu as pltpu
from jax.sharding import PartitionSpec as P

SIDE = 128
HALF = 8
SLOTS = 16
ROWS = 64
CUT_LIMIT = 16
CELLS = SIDE * SIDE
BITS = (0, 5)

f32 = jnp.float32
bf16 = jnp.bfloat16


def fourier_tables():
    index = np.arange(SIDE)
    angle = (np.outer(index, index) % SIDE) * (2.0 * math.pi / SIDE)
    cosine, sine = np.cos(angle), np.sin(angle)

    def pieces(table):
        high = table.astype(ml_dtypes.bfloat16)
        low = (table - high.astype(np.float64)).astype(ml_dtypes.bfloat16)
        return high, low

    cos_high, cos_low = pieces(cosine)
    sin_high, sin_low = pieces(sine)
    first = np.block([[cos_high, sin_high], [cos_low, sin_low]])
    left_high = np.block([[cos_high, -sin_high], [sin_high, cos_high]])
    left_low = np.block([[cos_low, -sin_low], [sin_low, cos_low]])
    left = np.concatenate([left_high, left_low, left_high], axis=1)
    right = np.concatenate([left_high.T, left_high.T, left_low.T], axis=0)
    return first, left, right


def tile_side(bit):
    return (lax.axis_index("tiles") >> bit) & 1


def cut_kernel(
    colour_ref, corner_ref, strips_ref, send_early, send_late, own_early, own_late, held, sems
):
    count = held.shape[1] // ROWS
    plans = []
    for r in range(2):
        plan = []
        for i in range(count):
            rows = pl.ds(i * ROWS, ROWS)
            copy = pltpu.make_async_copy(
                strips_ref.at[colour_ref[0, r], rows], held.at[r, rows], sems.at[r, i]
            )
            copy.start()
            plan.append(copy)
        plans.append(plan)
    last = held.shape[2] // SIDE - 1
    rows = lax.broadcasted_iota(jnp.int32, (SIDE, SIDE), 0)
    lanes = lax.broadcasted_iota(jnp.int32, (SIDE, SIDE), 1)
    for r, outs in enumerate(((send_early, own_early), (send_late, own_late))):
        for copy in plans[r]:
            copy.wait()
        side = tile_side(BITS[r])
        for out_ref, start in zip(outs, (HALF - HALF * side, HALF * side)):
            for j in range(HALF):
                row = corner_ref[0, r, 0, start + j]
                col = corner_ref[0, r, 1, start + j]
                block = col >> 7
                shift = col - block * SIDE
                halves = []
                for b in (block, jnp.minimum(block + 1, last)):
                    at = pl.ds(pl.multiple_of(b * SIDE, SIDE), SIDE)
                    top = held[r, :SIDE, at].astype(f32)
                    bottom = held[r, SIDE:, at].astype(f32)
                    halves.append(jnp.where(rows >= row, top, bottom))
                out_ref[j] = jnp.where(lanes >= shift, *halves).astype(bf16)


scalars = pl.BlockSpec(memory_space=pltpu.SMEM)
vectors = pl.BlockSpec(memory_space=pltpu.VMEM)
far_memory = pl.BlockSpec(memory_space=pltpu.HBM)


def cut(colour, corners, strips):
    windows = jax.ShapeDtypeStruct((HALF, SIDE, SIDE), bf16)
    return pl.pallas_call(
        cut_kernel,
        out_shape=(windows,) * 4,
        in_specs=[scalars, scalars, far_memory],
        out_specs=(vectors,) * 4,
        scratch_shapes=[
            pltpu.VMEM(strips.shape, bf16),
            pltpu.SemaphoreType.DMA((2, strips.shape[1] // ROWS)),
        ],
        compiler_params=pltpu.CompilerParams(vmem_limit_bytes=CUT_LIMIT * 1024 * 1024),
        cost_estimate=pl.CostEstimate(
            flops=4 * HALF * CELLS * 8, bytes_accessed=4 * HALF * CELLS * 10, transcendentals=0
        ),
    )(colour, corners, strips)


def split(x):
    high = x.astype(bf16)
    return high, (x - high.astype(f32)).astype(bf16)


def matmul(a, b):
    return jnp.dot(a, b, preferred_element_type=f32)


def left_mul(table, x):
    high, low = split(x)
    return matmul(table, jnp.concatenate([high, high, low], axis=0))


def right_mul(x, table):
    high, low = split(x)
    return matmul(jnp.concatenate([high, low, high], axis=1), table)


def forward_pair(first_window, second_window, first, left):
    parts = []
    for window in (first_window, second_window):
        parts.append(matmul(jnp.concatenate([window, window], axis=1), first))
    a, b = parts
    stacked = jnp.concatenate(
        [
            jnp.concatenate([a[:, :SIDE], b[:, :SIDE]], axis=1),
            jnp.concatenate([a[:, SIDE:], b[:, SIDE:]], axis=1),
        ],
        axis=0,
    )
    return left_mul(left, stacked)


def near_kernel(own_early, own_late, first_ref, left_ref, early_ref, late_ref):
    for window_ref, out_ref in ((own_early, early_ref), (own_late, late_ref)):
        for q in range(HALF // 2):
            out_ref[q] = forward_pair(
                window_ref[2 * q], window_ref[2 * q + 1], first_ref[...], left_ref[...]
            )


def near_spectra(own_early, own_late, first, left):
    shape = jax.ShapeDtypeStruct((HALF // 2, 2 * SIDE, 2 * SIDE), f32)
    return pl.pallas_call(
        near_kernel,
        out_shape=(shape, shape),
        in_specs=[vectors] * 4,
        out_specs=(vectors, vectors),
        compiler_params=pltpu.CompilerParams(vmem_limit_bytes=32 * 1024 * 1024),
        cost_estimate=pl.CostEstimate(
            flops=SLOTS * 8 * 2 * SIDE**3 * 2, bytes_accessed=SLOTS * CELLS * 10, transcendentals=0
        ),
    )(own_early, own_late, first, left)


def total(x):
    return jnp.sum(jnp.sum(x, axis=0, keepdims=True), axis=1, keepdims=True)


def correlate_group(near, windows, first_ref, left_ref, right_ref, place, plain, ramp, edge):
    spectra = []
    for q in range(2):
        here = near[q]
        far = forward_pair(windows[2 * q], windows[2 * q + 1], first_ref[...], left_ref[...])
        near_real, near_imag = here[:SIDE], here[SIDE:]
        far_real, far_imag = far[:SIDE], far[SIDE:]
        cross_real = near_real * far_real + near_imag * far_imag
        cross_imag = near_real * far_imag - near_imag * far_real
        square = cross_real * cross_real + cross_imag * cross_imag
        magnitude = jnp.sqrt(square)
        whites = []
        for h in range(2):
            part = slice(h * SIDE, (h + 1) * SIDE)
            size = magnitude[:, part]
            scale = 1.0 / (size + (total(size) * (0.1 / CELLS) + 1e-6))
            whites.append((cross_real[:, part] * scale, cross_imag[:, part] * scale))
        (a_real, a_imag), (b_real, b_imag) = whites
        spectra.append((a_real - b_imag, a_imag + b_real))
    stacked = jnp.concatenate(
        [
            jnp.concatenate([spectra[0][0], spectra[1][0]], axis=1),
            jnp.concatenate([spectra[0][1], spectra[1][1]], axis=1),
        ],
        axis=0,
    )
    back = left_mul(left_ref[...], stacked)
    rows = jnp.concatenate(
        [
            jnp.concatenate([back[:SIDE, :SIDE], back[SIDE:, :SIDE]], axis=1),
            jnp.concatenate([back[:SIDE, SIDE:], back[SIDE:, SIDE:]], axis=1),
        ],
        axis=0,
    )
    surfaces = right_mul(rows, right_ref[...])
    row_index = lax.broadcasted_iota(jnp.int32, (SIDE, SIDE), 0)
    row_coord = (((row_index + SIDE // 2) & (SIDE - 1)) - SIDE // 2).astype(f32)
    for p in range(4):
        q, h = divmod(p, 2)
        surface = surfaces[q * SIDE : (q + 1) * SIDE, h * SIDE : (h + 1) * SIDE]
        mean = total(surface) * (1.0 / CELLS)
        variance = total(surface * surface) * (1.0 / CELLS) - mean * mean
        peak = jnp.max(jnp.max(surface, axis=0, keepdims=True), axis=1, keepdims=True)
        spread = jnp.sqrt(jnp.maximum(variance, 0.0) * (1.0 / CELLS**2) + 1e-6)
        factor = (2.0 / CELLS) / spread
        weight = jnp.exp((surface - peak) * factor)
        at = slice(place + p, place + p + 1)
        plain[at, :] = jnp.sum(weight, axis=0, keepdims=True)
        ramp[at, :] = jnp.sum(weight * row_coord, axis=0, keepdims=True)
        edge[at, :] = weight[SIDE // 2 : SIDE // 2 + 1, :]


def correlate_groups(near_ref, window_ref, tables, sums):
    for g in range(HALF // 4):
        near = [near_ref[2 * g + q] for q in range(2)]
        windows = [window_ref[4 * g + p] for p in range(4)]
        correlate_group(near, windows, *tables, 4 * g, *sums)


def early_kernel(near_ref, window_ref, first_ref, left_ref, right_ref, out_ref):
    sums = [out_ref.at[i] for i in range(3)]
    correlate_groups(near_ref, window_ref, (first_ref, left_ref, right_ref), sums)


def late_kernel(
    live_ref, ids_ref, early_ref, near_ref, window_ref, first_ref, left_ref, right_ref, out_ref, late
):
    sums = [late.at[i] for i in range(3)]
    correlate_groups(near_ref, window_ref, (first_ref, left_ref, right_ref), sums)
    lane = lax.broadcasted_iota(jnp.int32, (8, SIDE), 1)
    sublane = lax.broadcasted_iota(jnp.int32, (8, SIDE), 0)
    coord = (((lane + SIDE // 2) & (SIDE - 1)) - SIDE // 2).astype(f32)
    chosen = jnp.where(lane == SIDE // 2, 1.0, 0.0)
    query = jnp.where(sublane == 0, 1.0, jnp.where(sublane == 1, coord, chosen))

    def reduce(i):
        both = jnp.concatenate([early_ref[i], late[i]], axis=0)
        return lax.dot_general(
            query,
            both,
            (((1,), (1,)), ((), ())),
            precision=lax.Precision.HIGHEST,
            preferred_element_type=f32,
        )

    plain_sums, ramp_sums, edge_sums = (reduce(i) for i in range(3))
    inverse = 1.0 / plain_sums[0:1]
    scale = 8.0 / SIDE
    row_shift = ramp_sums[0:1] * inverse * scale
    col_shift = plain_sums[1:2] * inverse * scale
    row_other = -row_shift - edge_sums[0:1] * inverse * (SIDE * scale)
    col_other = -col_shift - plain_sums[2:3] * inverse * (SIDE * scale)
    slot = lax.broadcasted_iota(jnp.int32, (1, SLOTS), 1)
    pieces = []
    for r in range(2):
        ids = jnp.where(slot < live_ref[0, r], ids_ref[0, r : r + 1, :], -1)
        pieces.append(ids.astype(f32))
    pieces += [row_shift, col_shift, row_other, col_other]
    pieces.append(jnp.zeros((1, SIDE - 6 * SLOTS), f32))
    row = jnp.concatenate(pieces, axis=1)
    out_ref[...] = jnp.broadcast_to(row, (SIDE, SIDE))


def correlate_cost(count):
    return pl.CostEstimate(
        flops=count * 12 * 2 * SIDE**3 * 2,
        bytes_accessed=count * CELLS * 10,
        transcendentals=count * CELLS * 3,
    )


def correlate_early(near, windows, tables):
    return pl.pallas_call(
        early_kernel,
        out_shape=jax.ShapeDtypeStruct((3, HALF, SIDE), f32),
        in_specs=[vectors] * 5,
        out_specs=vectors,
        compiler_params=pltpu.CompilerParams(vmem_limit_bytes=32 * 1024 * 1024),
        cost_estimate=correlate_cost(HALF),
    )(near, windows, *tables)


def correlate_late(live, ids, early, near, windows, tables):
    return pl.pallas_call(
        late_kernel,
        out_shape=jax.ShapeDtypeStruct((SIDE, SIDE), f32),
        in_specs=[scalars] + [vectors] * 7,
        out_specs=vectors,
        scratch_shapes=[pltpu.VMEM((3, HALF, SIDE), f32)],
        compiler_params=pltpu.CompilerParams(vmem_limit_bytes=32 * 1024 * 1024),
        cost_estimate=correlate_cost(HALF),
    )(live, ids, early, near, windows, *tables)


def collect_kernel(packed_ref, out_ref):
    packed = packed_ref[...].T
    base = (lax.axis_index("tiles") * lax.axis_size("grp") + lax.axis_index("grp")) * SIDE
    device = lax.broadcasted_iota(jnp.int32, (HALF, SIDE), 1)
    node = lax.broadcasted_iota(jnp.int32, (SIDE, SIDE), 0).astype(f32)
    sums = [jnp.zeros((SIDE, SIDE), f32), jnp.zeros((SIDE, SIDE), f32)]
    for r, bit in enumerate(BITS):
        reach = 2 << bit
        side = (device >> (bit + 1)) & 1
        own, other = [], []
        for c in range(2):
            own.append(packed[32 + 16 * c + HALF * r :][:HALF])
            far = packed[64 + 16 * c + HALF * r :][:HALF]
            up = pltpu.roll(far, SIDE - reach, 1)
            down = pltpu.roll(far, reach, 1)
            other.append(jnp.where(side == 0, up, down))
        for h in range(2):
            local = packed[SLOTS * r + HALF * h :][:HALF] - base.astype(f32)
            values = [jnp.where(side == h, own[c], other[c]) for c in range(2)]
            for j in range(HALF):
                hit = node == local[j : j + 1]
                for c in range(2):
                    sums[c] = sums[c] + jnp.where(hit, values[c][j : j + 1], 0.0)
    ones = jnp.ones((8, SIDE), f32)
    for c in range(2):
        summed = lax.dot_general(
            ones,
            sums[c],
            (((1,), (1,)), ((), ())),
            precision=lax.Precision.HIGHEST,
            preferred_element_type=f32,
        )
        out_ref[c : c + 1] = summed[0:1]


def collect(packed):
    return pl.pallas_call(
        collect_kernel,
        out_shape=jax.ShapeDtypeStruct((2, SIDE), f32),
        in_specs=[pl.BlockSpec(memory_space=pltpu.VMEM)],
        out_specs=pl.BlockSpec(memory_space=pltpu.VMEM),
    )(packed)


def swap(x, bit):
    pairs = [(i, i ^ (1 << bit)) for i in range(lax.axis_size("tiles"))]
    return lax.ppermute(x, "tiles", pairs)


def on_device(strips, edge_colour, patch_offsets, patch_live, node_ids):
    tables = [jnp.asarray(table) for table in fourier_tables()]
    corners = jnp.transpose(patch_offsets, (0, 1, 3, 2))
    strips = pltpu.with_memory_space_constraint(strips, pltpu.HBM)
    send_early, send_late, own_early, own_late = cut(edge_colour, corners, strips)
    far_early = swap(send_early, BITS[0])
    far_late = swap(send_late, BITS[1])
    near_early, near_late = near_spectra(own_early, own_late, *tables[:2])
    early = correlate_early(near_early, far_early, tables)
    packed = correlate_late(patch_live, node_ids, early, near_late, far_late, tables)
    packed = packed.reshape(SIDE, 1, SIDE)
    gathered = lax.all_to_all(packed, ("tiles", "grp"), 0, 0, tiled=True)
    return collect(gathered.reshape(SIDE, SIDE))


def solution(mesh):
    placed = (
        P(("tiles", "grp"), None, None),
        P(("tiles", "grp"), None),
        P(("tiles", "grp"), None, None, None),
        P(("tiles", "grp"), None),
        P(("tiles", "grp"), None, None),
    )
    return jax.shard_map(
        on_device, mesh=mesh, in_specs=placed, out_specs=P(None, ("tiles", "grp")), check_vma=False
    )
```

time: 52.2 us -> 43.1 us (0.83)
  local copies, waits for them, and re-layouts: 8.04 us -> 1.36 us
  Pallas kernels: 19.3 us -> 14.1 us
  blocking collectives: 17.7 us -> 20.9 us
  other arithmetic: 0.94 us -> 0 us
  waiting for transfers between devices: 0.01 us -> 0.87 us
    pallas_call x5 -> x4, Pallas kernels: 17 us -> 11.8 us  [the longest x1 3.64 us: correlate_late(): pl.pallas_call(late_kernel, out_shape=jax.ShapeDtypeStruct((SIDE, SIDE),...]
    unnamed x15 -> x14, local copies, waits for them, and re-layouts: 6.61 us -> 1.36 us
    all_to_all x1, blocking collectives: 17.7 us -> 20.9 us  [on_device(): gathered = lax.all_to_all(packed, ('tiles', 'grp'), 0, 0, tiled=True)]
    ppermute x2, waiting for transfers between devices: 0.01 us -> 0.87 us  [swap(): return lax.ppermute(x, 'tiles', pairs)]
    concatenate x1 -> x0, other arithmetic: 0.86 us -> none  [on_device(): far = jnp.concatenate([far_early, far_late], axis=0)]
    broadcast_in_dim x1 -> x0, local copies, waits for them, and re-layouts: 0.64 us -> none  [on_device(): spread = jnp.broadcast_to(packed, (SIDE, SIDE))]
  transfers between devices with their start and end apart: 2 -> 2, of which waited for: 0 -> 1; matrix products, arithmetic and copies ran while one was open for 1% -> 0% of each run, Pallas kernels for 14% -> 11%
where the time goes in v2:
time: 43.1 us; the launch traced here: 42.9 us
  blocking collectives  20.9 us (48%)
  Pallas kernels  14.1 us (33%)
  starting transfers between devices  5.72 us (13%)
  local copies, waits for them, and re-layouts  1.36 us (3%)
  waiting for transfers between devices  0.87 us (2%)
    all_to_all x1, blocking collectives, on_device(): gathered = lax.all_to_all(packed, ('tiles', 'grp'), 0, 0, tiled=True)  20.9 us
    ppermute x2, starting transfers between devices, swap(): return lax.ppermute(x, 'tiles', pairs)  5.72 us
    pallas_call x1, Pallas kernels, correlate_late(): pl.pallas_call(late_kernel, out_shape=jax.ShapeDtypeStruct((SIDE, SIDE),...  3.64 us
    pallas_call x1, Pallas kernels, cut(): pl.pallas_call(cut_kernel, out_shape=(windows,) * 4, in_specs=[scalars, s...  3.33 us
    pallas_call x1, Pallas kernels, correlate_early(): pl.pallas_call(early_kernel, out_shape=jax.ShapeDtypeStruct((3, HALF, SID...  2.95 us
    pallas_call x1, Pallas kernels, collect(): pl.pallas_call(collect_kernel, out_shape=jax.ShapeDtypeStruct((2, SIDE),...  2.27 us
    pallas_call x1, Pallas kernels, near_spectra(): pl.pallas_call(near_kernel, out_shape=(shape, shape), in_specs=[vectors]...  1.87 us
    unnamed x14, local copies, waits for them, and re-layouts  1.36 us
  transfers between devices with their start and end apart: 2, of which 1 were waited for; matrix products, arithmetic and copies ran while one was open for 0% of the time, Pallas kernels for 11%

profile of v2, /device:TPU:1, one launch (start us, length us, event | category | flops | bytes accessed | tf_op | source)
XLA Modules:
  0.0 42.9 jit_solution(11937317200645974370)
XLA Ops:
  0.0 0.0 copy-start
  0.0 0.7 %copy-done = s32[1,2,16,2]{2,3,1,0:T(2,128)S(1)} copy-done((s32[1,2,16,2]{2,3,1,0:T(2,128)S(1)}, s32[1,2,16,2]{2,3,1,0:T(2,128)}, u32[]{:S(2)}) %copy-start) | copy-done | bytes 280
  0.7 0.0 copy-start.1
  0.7 0.7 %copy-done.1 = s32[1,2]{1,0:T(1,128)S(1)} copy-done((s32[1,2]{1,0:T(1,128)S(1)}, s32[1,2]{1,0:T(1,128)}, u32[]{:S(2)}) %copy-start.1) | copy-done | bytes 32
  1.3 0.0 copy-start.4
  1.3 0.0 copy-start.6
  1.3 0.0 copy-start.5
  1.3 3.3 %shard_map.82 = (bf16[8,128,128]{2,1,0:T(8,128)(2,1)S(1)}, bf16[8,128,128]{2,1,0:T(8,128)(2,1)S(1)}, bf16[8,128,128]{2,1,0:T(8,128)(2,1)S(1)}, bf16[8,128,128]{2,1,0:T(8,128)(2,1)S(1)}) custom-call(s32[1,2]{1,0:T(1,128)S(1)} %copy-done.1, s32[1,2,2,16]{3,2,1,0:T(2,128)S(1)} %bitcast.6, bf16[2,256,4096]{2,1,0:T(8,128)(2,1)} %strips_ref.1), custom_call_target="tpu_custom_call" | custom-call | flops 4194304 | bytes 5242880 | tf_op jit(solution)/shard_map/pallas_call | solution.py:93
  4.7 0.0 copy-start.2
  4.7 0.0 copy-start.3
  4.7 2.1 %collective-permute-start = (bf16[8,128,128]{2,1,0:T(8,128)(2,1)S(1)}, bf16[8,128,128]{2,1,0:T(8,128)(2,1)S(1)}, u32[]{:S(2)}, u32[]{:S(2)}) collective-permute-start(bf16[8,128,128]{2,1,0:T(8,128)(2,1)S(1)} %get-tuple-element.14), channel_id=1, source_target_pairs={{0,2},{2,0},{4,6},{6,4},{8,10},{10,8},{12,14},{14,12},{16,18},{18,... | collective-permute-start | bytes 786440 | tf_op jit(solution)/shard_map/ppermute | solution.py:349
  6.8 3.6 %collective-permute-start.1 = (bf16[8,128,128]{2,1,0:T(8,128)(2,1)S(1)}, bf16[8,128,128]{2,1,0:T(8,128)(2,1)S(1)}, u32[]{:S(2)}, u32[]{:S(2)}) collective-permute-start(bf16[8,128,128]{2,1,0:T(8,128)(2,1)S(1)} %get-tuple-element.16), channel_id=1, source_target_pairs={{0,64},{2,66},{4,68},{6,70},{8,72},{10,74},{12,76},{14,78},{16,80}... | collective-permute-start | bytes 786440 | tf_op jit(solution)/shard_map/ppermute | solution.py:349
  10.4 0.0 copy-done.4
  10.4 0.0 copy-done.6
  10.4 1.9 %shard_map.83 = (f32[4,256,256]{2,1,0:T(8,128)S(1)}, f32[4,256,256]{2,1,0:T(8,128)S(1)}) custom-call(bf16[8,128,128]{2,1,0:T(8,128)(2,1)S(1)} %get-tuple-element.11.own_early, bf16[8,128,128]{2,1,0:T(8,128)(2,1)S(1)} %get-tuple-element.12.own_late, bf16[256,256]{1,0:T(8,128)(2,1)S(1)} %copy-done.6, bf16[256,768]{1,0:T(8,128)(2,1)S(1)} %copy-done.4), custom_call_target="tpu_custom_call" | custom-call | flops 1073741824 | bytes 2621440 | tf_op jit(solution)/shard_map/pallas_call | solution.py:153
  12.3 0.0 collective-permute-done.window_ref
  12.4 0.0 copy-done.5
  12.4 3.0 %shard_map.84.early_ref = f32[3,8,128]{2,1,0:T(8,128)S(1)} custom-call(f32[4,256,256]{2,1,0:T(8,128)S(1)} %get-tuple-element.13.near_ref, bf16[8,128,128]{2,1,0:T(8,128)(2,1)S(1)} %collective-permute-done.window_ref, bf16[256,256]{1,0:T(8,128)(2,1)S(1)} %copy-done.6, bf16[256,768]{1,0:T(8,128)(2,1)S(1)} %copy-done.4, bf16[768,256]{1,0:T(8,128)(2,1)S(1)} %copy-done.5), custom_call_target="tpu_custom_call" | custom-call | flops 805306368 | bytes 1310720 | tf_op jit(solution)/shard_map/pallas_call | solution.py:281
  15.3 0.8 %collective-permute-done.1.window_ref = bf16[8,128,128]{2,1,0:T(8,128)(2,1)S(1)} collective-permute-done((bf16[8,128,128]{2,1,0:T(8,128)(2,1)S(1)}, bf16[8,128,128]{2,1,0:T(8,128)(2,1)S(1)}, u32[]{:S(2)}, u32[]{:S(2)}) %collective-permute-start.1) | collective-permute-done | bytes 262176 | tf_op jit(solution)/shard_map/ppermute | solution.py:349
  16.1 0.0 copy-done.2
  16.1 0.0 copy-done.3
  16.1 3.6 %shard_map.85 = f32[128,128]{1,0:T(8,128)S(1)} custom-call(s32[1,2]{1,0:T(1,128)S(1)} %copy-done.3, s32[1,2,16]{2,1,0:T(2,128)S(1)} %copy-done.2, f32[3,8,128]{2,1,0:T(8,128)S(1)} %shard_map.84.early_ref, f32[4,256,256]{2,1,0:T(8,128)S(1)} %get-tuple-element.15.near_ref, bf16[8,128,128]{2,1,0:T(8,128)(2,1)S(1)} %collective-permute-done.1.window_ref, ...), custom_call_target="tpu_custom_call" | custom-call | flops 805306368 | bytes 1310720 | tf_op jit(solution)/shard_map/pallas_call | solution.py:292
  19.8 20.9 %all_to_all.5 = f32[128,1,128]{2,1,0:T(1,128)} all-to-all(f32[128,1,128]{2,1,0:T(1,128)S(1)} %bitcast.5), channel_id=1, replica_groups=mesh['tiles'=64,'grp'=2] {'tiles','grp'}, dimensions={0} | all-to-all | bytes 131072 | tf_op jit(solution)/shard_map/all_to_all | solution.py:363
  40.6 2.3 %shard_map.86 = f32[2,128]{1,0:T(2,128)} custom-call(f32[128,128]{1,0:T(8,128)} %bitcast.7), custom_call_target="tpu_custom_call" | custom-call | tf_op jit(solution)/shard_map/pallas_call | solution.py:339
Async XLA Ops:
  0.0 0.7 %copy-start = (s32[1,2,16,2]{2,3,1,0:T(2,128)S(1)}, s32[1,2,16,2]{2,3,1,0:T(2,128)}, u32[]{:S(2)}) copy-start(s32[1,2,16,2]{2,3,1,0:T(2,128)} %param.10) | copy-start | bytes 772
  0.7 0.7 %copy-start.1 = (s32[1,2]{1,0:T(1,128)S(1)}, s32[1,2]{1,0:T(1,128)}, u32[]{:S(2)}) copy-start(s32[1,2]{1,0:T(1,128)} %colour_ref.1) | copy-start | bytes 28
  1.3 9.1 %copy-start.4 = (bf16[256,768]{1,0:T(8,128)(2,1)S(1)}, bf16[256,768]{1,0:T(8,128)(2,1)}, u32[]{:S(2)}) copy-start(bf16[256,768]{1,0:T(8,128)(2,1)} %constant.7.clone.left_ref) | copy-start | bytes 1179652
  1.3 9.1 %copy-start.6 = (bf16[256,256]{1,0:T(8,128)(2,1)S(1)}, bf16[256,256]{1,0:T(8,128)(2,1)}, u32[]{:S(2)}) copy-start(bf16[256,256]{1,0:T(8,128)(2,1)} %constant.6.clone.first_ref) | copy-start | bytes 393220
  1.3 11.0 %copy-start.5 = (bf16[768,256]{1,0:T(8,128)(2,1)S(1)}, bf16[768,256]{1,0:T(8,128)(2,1)}, u32[]{:S(2)}) copy-start(bf16[768,256]{1,0:T(8,128)(2,1)} %constant.8.clone.right_ref) | copy-start | bytes 1179652
  4.7 11.5 %copy-start.2 = (s32[1,2,16]{2,1,0:T(2,128)S(1)}, s32[1,2,16]{2,1,0:T(2,128)}, u32[]{:S(2)}) copy-start(s32[1,2,16]{2,1,0:T(2,128)} %ids_ref.1) | copy-start | bytes 388
  4.7 11.4 %copy-start.3 = (s32[1,2]{1,0:T(1,128)S(1)}, s32[1,2]{1,0:T(1,128)}, u32[]{:S(2)}) copy-start(s32[1,2]{1,0:T(1,128)} %live_ref.1) | copy-start | bytes 28
  4.7 7.6 %collective-permute-start = (bf16[8,128,128]{2,1,0:T(8,128)(2,1)S(1)}, bf16[8,128,128]{2,1,0:T(8,128)(2,1)S(1)}, u32[]{:S(2)}, u32[]{:S(2)}) collective-permute-start(bf16[8,128,128]{2,1,0:T(8,128)(2,1)S(1)} %get-tuple-element.14), channel_id=1, source_target_pairs={{0,2},{2,0},{4,6},{6,4},{8,10},{10,8},{12,14},{14,12},{16,18},{18,... | collective-permute-start | bytes 786440 | tf_op jit(solution)/shard_map/ppermute | solution.py:349
  6.8 9.3 %collective-permute-start.1 = (bf16[8,128,128]{2,1,0:T(8,128)(2,1)S(1)}, bf16[8,128,128]{2,1,0:T(8,128)(2,1)S(1)}, u32[]{:S(2)}, u32[]{:S(2)}) collective-permute-start(bf16[8,128,128]{2,1,0:T(8,128)(2,1)S(1)} %get-tuple-element.16), channel_id=1, source_target_pairs={{0,64},{2,66},{4,68},{6,70},{8,72},{10,74},{12,76},{14,78},{16,80}... | collective-permute-start | bytes 786440 | tf_op jit(solution)/shard_map/ppermute | solution.py:349

commit v3 on v2

v3 whole, which is shorter than its diff:
```python
import functools
import math

import jax
import jax.numpy as jnp
import ml_dtypes
import numpy as np
from jax import lax
from jax.experimental import pallas as pl
from jax.experimental.pallas import tpu as pltpu
from jax.sharding import PartitionSpec as P

SIDE = 128
HALF = 8
SLOTS = 16
ROWS = 64
CELLS = SIDE * SIDE
BITS = (0, 5)

f32 = jnp.float32
bf16 = jnp.bfloat16


def fourier_tables():
    index = np.arange(SIDE)
    angle = (np.outer(index, index) % SIDE) * (2.0 * math.pi / SIDE)
    cosine, sine = np.cos(angle), np.sin(angle)

    def pieces(table):
        high = table.astype(ml_dtypes.bfloat16)
        low = (table - high.astype(np.float64)).astype(ml_dtypes.bfloat16)
        return high, low

    cos_high, cos_low = pieces(cosine)
    sin_high, sin_low = pieces(sine)
    first = np.block([[cos_high, sin_high], [cos_low, sin_low]])
    left_high = np.block([[cos_high, -sin_high], [sin_high, cos_high]])
    left_low = np.block([[cos_low, -sin_low], [sin_low, cos_low]])
    second = np.concatenate([left_high.T, left_high.T, left_low.T], axis=0)
    return first, second


def tile_side(bit):
    return (lax.axis_index("tiles") >> bit) & 1


def cut_windows(r, mine, colour_ref, corner_ref, held_ref):
    last = held_ref.shape[2] // SIDE - 1
    rows = lax.broadcasted_iota(jnp.int32, (SIDE, SIDE), 0)
    lanes = lax.broadcasted_iota(jnp.int32, (SIDE, SIDE), 1)
    colour = colour_ref[0, r]
    side = tile_side(BITS[r])
    start = HALF * side if mine else HALF - HALF * side
    for j in range(HALF):
        row = corner_ref[0, r, 0, start + j]
        col = corner_ref[0, r, 1, start + j]
        block = col >> 7
        shift = col - block * SIDE
        halves = []
        for b in (block, jnp.minimum(block + 1, last)):
            at = pl.ds(pl.multiple_of(b * SIDE, SIDE), SIDE)
            top = held_ref[colour, :SIDE, at].astype(f32)
            bottom = held_ref[colour, SIDE:, at].astype(f32)
            halves.append(jnp.where(rows >= row, top, bottom))
        yield jnp.where(lanes >= shift, *halves).astype(bf16)


def hold_kernel(
    colour_hbm, corner_hbm, strips_ref, held_ref, send_ref, colour_ref, corner_ref, sems, small_sems
):
    small = [
        pltpu.make_async_copy(colour_hbm, colour_ref, small_sems.at[0]),
        pltpu.make_async_copy(corner_hbm, corner_ref, small_sems.at[1]),
    ]
    large = []
    for i in range(strips_ref.shape[0]):
        for j in range(strips_ref.shape[1] // ROWS):
            rows = pl.ds(j * ROWS, ROWS)
            large.append(
                pltpu.make_async_copy(strips_ref.at[i, rows], held_ref.at[i, rows], sems.at[i, j])
            )
    for copy in small + large:
        copy.start()
    for copy in small + large:
        copy.wait()
    for j, window in enumerate(cut_windows(0, False, colour_ref, corner_ref, held_ref)):
        send_ref[j] = window


def send_kernel(colour_ref, corner_ref, held_ref, send_ref):
    for j, window in enumerate(cut_windows(1, False, colour_ref, corner_ref, held_ref)):
        send_ref[j] = window


scalars = pl.BlockSpec(memory_space=pltpu.SMEM)
vectors = pl.BlockSpec(memory_space=pltpu.VMEM)
far_memory = pl.BlockSpec(memory_space=pltpu.HBM)


def cut_cost(bytes_accessed):
    return pl.CostEstimate(
        flops=HALF * CELLS * 8, bytes_accessed=bytes_accessed, transcendentals=0
    )


def hold(colour, corners, strips):
    return pl.pallas_call(
        hold_kernel,
        out_shape=(
            jax.ShapeDtypeStruct(strips.shape, bf16),
            jax.ShapeDtypeStruct((HALF, SIDE, SIDE), bf16),
        ),
        in_specs=[far_memory] * 3,
        out_specs=(vectors, vectors),
        scratch_shapes=[
            pltpu.SMEM(colour.shape, jnp.int32),
            pltpu.SMEM(corners.shape, jnp.int32),
            pltpu.SemaphoreType.DMA((2, strips.shape[1] // ROWS)),
            pltpu.SemaphoreType.DMA((2,)),
        ],
        compiler_params=pltpu.CompilerParams(vmem_limit_bytes=16 * 1024 * 1024),
        cost_estimate=cut_cost(2 * strips.size),
    )(*(pltpu.with_memory_space_constraint(x, pltpu.HBM) for x in (colour, corners, strips)))


def cut_late(colour, corners, held):
    return pl.pallas_call(
        send_kernel,
        out_shape=jax.ShapeDtypeStruct((HALF, SIDE, SIDE), bf16),
        in_specs=[scalars, scalars, vectors],
        out_specs=vectors,
        compiler_params=pltpu.CompilerParams(vmem_limit_bytes=16 * 1024 * 1024),
        cost_estimate=cut_cost(HALF * CELLS * 2),
    )(colour, corners, held)


def split(x):
    high = x.astype(bf16)
    return high, (x - high.astype(f32)).astype(bf16)


def matmul(a, b):
    return jnp.dot(a, b, preferred_element_type=f32)


def second_mul(high, low, second):
    return matmul(jnp.concatenate([high, low, high], axis=1), second)


def turned(x):
    blocks = []
    for i in range(x.shape[0] // SIDE):
        rows = x[i * SIDE : (i + 1) * SIDE]
        blocks.append(jnp.concatenate([rows[:, :SIDE].T, rows[:, SIDE:].T], axis=1))
    return jnp.concatenate(blocks, axis=0)


def forward(windows, first, second):
    rows = matmul(jnp.concatenate([windows, windows], axis=1), first)
    high, low = split(rows)
    return second_mul(turned(high), turned(low), second)


def near_kernel(colour_ref, corner_ref, held_ref, first_ref, second_ref, early_ref, late_ref):
    for r, out_ref in enumerate((early_ref, late_ref)):
        windows = jnp.concatenate(
            list(cut_windows(r, True, colour_ref, corner_ref, held_ref)), axis=0
        )
        out_ref[...] = forward(windows, first_ref[...], second_ref[...])


def near_spectra(colour, corners, held, first, second):
    shape = jax.ShapeDtypeStruct((HALF * SIDE, 2 * SIDE), f32)
    return pl.pallas_call(
        near_kernel,
        out_shape=(shape, shape),
        in_specs=[scalars, scalars] + [vectors] * 3,
        out_specs=(vectors, vectors),
        compiler_params=pltpu.CompilerParams(vmem_limit_bytes=32 * 1024 * 1024),
        cost_estimate=pl.CostEstimate(
            flops=SLOTS * 8 * 2 * SIDE**3 * 2, bytes_accessed=SLOTS * CELLS * 10, transcendentals=0
        ),
    )(colour, corners, held, first, second)


def patch_rows(x, p):
    return x[p * SIDE : (p + 1) * SIDE]


def down(x):
    return jnp.sum(x, axis=0, keepdims=True)


def across(rows):
    return jnp.sum(jnp.concatenate(rows, axis=0), axis=1, keepdims=True)


def correlate_group(near_ref, window_ref, first_ref, second_ref, sums_ref):
    far = forward(window_ref[...].reshape(HALF * SIDE, SIDE), first_ref[...], second_ref[...])
    crosses, sizes, size_rows = [], [], []
    for p in range(HALF):
        here, there = near_ref[p * SIDE : (p + 1) * SIDE, :], patch_rows(far, p)
        near_real, near_imag = here[:, :SIDE], here[:, SIDE:]
        far_real, far_imag = there[:, :SIDE], there[:, SIDE:]
        real = near_real * far_real + near_imag * far_imag
        imag = near_real * far_imag - near_imag * far_real
        size = jnp.sqrt(real * real + imag * imag)
        crosses.append((real, imag))
        sizes.append(size)
        size_rows.append(down(size))
    floors = across(size_rows) * (0.1 / CELLS) + 1e-6
    whites = []
    for p in range(HALF):
        scale = 1.0 / (sizes[p] + floors[p : p + 1])
        whites.append((crosses[p][0] * scale, crosses[p][1] * scale))
    spectra = []
    for q in range(HALF // 2):
        (a_real, a_imag), (b_real, b_imag) = whites[2 * q], whites[2 * q + 1]
        spectra.append(jnp.concatenate([a_real - b_imag, a_imag + b_real], axis=1))
    back = second_mul(*split(jnp.concatenate(spectra, axis=0)), second_ref[...])
    high, low = split(back)
    surfaces = second_mul(turned(high), turned(low), second_ref[...])
    patches = []
    for p in range(HALF):
        q, h = divmod(p, 2)
        patches.append(patch_rows(surfaces, q)[:, h * SIDE : (h + 1) * SIDE])
    mean = across([down(x) for x in patches]) * (1.0 / CELLS)
    square = across([down(x * x) for x in patches]) * (1.0 / CELLS)
    peak = jnp.max(
        jnp.concatenate([jnp.max(x, axis=0, keepdims=True) for x in patches], axis=0),
        axis=1,
        keepdims=True,
    )
    variance = jnp.maximum(square - mean * mean, 0.0)
    factor = (2.0 / CELLS) / jnp.sqrt(variance * (1.0 / CELLS**2) + 1e-6)
    row_index = lax.broadcasted_iota(jnp.int32, (SIDE, SIDE), 0)
    row_coord = (((row_index + SIDE // 2) & (SIDE - 1)) - SIDE // 2).astype(f32)
    for p, surface in enumerate(patches):
        weight = jnp.exp((surface - peak[p : p + 1]) * factor[p : p + 1])
        sums_ref[0, p : p + 1, :] = down(weight)
        sums_ref[1, p : p + 1, :] = down(weight * row_coord)
        sums_ref[2, p : p + 1, :] = weight[SIDE // 2 : SIDE // 2 + 1, :]


def late_kernel(
    live_ref, ids_ref, early_ref, near_ref, window_ref, first_ref, second_ref, out_ref, late_ref
):
    correlate_group(near_ref, window_ref, first_ref, second_ref, late_ref)
    lane = lax.broadcasted_iota(jnp.int32, (8, SIDE), 1)
    sublane = lax.broadcasted_iota(jnp.int32, (8, SIDE), 0)
    coord = (((lane + SIDE // 2) & (SIDE - 1)) - SIDE // 2).astype(f32)
    chosen = jnp.where(lane == SIDE // 2, 1.0, 0.0)
    query = jnp.where(sublane == 0, 1.0, jnp.where(sublane == 1, coord, chosen))
    terms = []
    for i in range(3):
        terms += [early_ref[i], late_ref[i]]
    sums = lax.dot_general(
        query,
        jnp.concatenate(terms, axis=0),
        (((1,), (1,)), ((), ())),
        precision=lax.Precision.HIGHEST,
        preferred_element_type=f32,
    )
    slot = lax.broadcasted_iota(jnp.int32, (1, SLOTS), 1)
    pieces = []
    for r in range(2):
        ids = jnp.where(slot < live_ref[0, r], ids_ref[0, r : r + 1, :], -1)
        pieces.append(ids.astype(f32))
    pieces += [sums[0:1], sums[1:2, :SLOTS], sums[2:3, :SLOTS]]
    pieces.append(jnp.zeros((1, SIDE - 7 * SLOTS), f32))
    out_ref[...] = jnp.broadcast_to(jnp.concatenate(pieces, axis=1), (SIDE, SIDE))


def correlate_cost(count):
    return pl.CostEstimate(
        flops=count * 12 * 2 * SIDE**3 * 2,
        bytes_accessed=count * CELLS * 10,
        transcendentals=count * CELLS * 3,
    )


def correlate_early(near, windows, tables):
    return pl.pallas_call(
        correlate_group,
        out_shape=jax.ShapeDtypeStruct((3, HALF, SIDE), f32),
        in_specs=[vectors] * 4,
        out_specs=vectors,
        compiler_params=pltpu.CompilerParams(vmem_limit_bytes=32 * 1024 * 1024),
        cost_estimate=correlate_cost(HALF),
    )(near, windows, *tables)


def correlate_late(live, ids, early, near, windows, tables):
    return pl.pallas_call(
        late_kernel,
        out_shape=jax.ShapeDtypeStruct((SIDE, SIDE), f32),
        in_specs=[scalars] + [vectors] * 6,
        out_specs=vectors,
        scratch_shapes=[pltpu.VMEM((3, HALF, SIDE), f32)],
        compiler_params=pltpu.CompilerParams(vmem_limit_bytes=32 * 1024 * 1024),
        cost_estimate=correlate_cost(HALF),
    )(live, ids, early, near, windows, *tables)


def collect_kernel(packed_ref, out_ref):
    packed = packed_ref[...].T
    base = (lax.axis_index("tiles") * lax.axis_size("grp") + lax.axis_index("grp")) * SIDE
    device = lax.broadcasted_iota(jnp.int32, (HALF, SIDE), 1)
    node = lax.broadcasted_iota(jnp.int32, (SIDE, SIDE), 0).astype(f32)
    sums = [jnp.zeros((SIDE, SIDE), f32), jnp.zeros((SIDE, SIDE), f32)]
    scale = 8.0 / SIDE
    for r, bit in enumerate(BITS):
        reach = 2 << bit
        side = (device >> (bit + 1)) & 1
        plain, ramp, edge, coord, chosen = (
            packed[2 * SLOTS + SLOTS * i + HALF * r :][:HALF] for i in range(5)
        )
        inverse = scale / plain
        own = [ramp * inverse, coord * inverse]
        other = []
        for shift, border in zip(own, (edge, chosen)):
            far = -shift - border * inverse * SIDE
            upper = pltpu.roll(far, SIDE - reach, 1)
            lower = pltpu.roll(far, reach, 1)
            other.append(jnp.where(side == 0, upper, lower))
        for h in range(2):
            local = packed[SLOTS * r + HALF * h :][:HALF] - base.astype(f32)
            values = [jnp.where(side == h, own[c], other[c]) for c in range(2)]
            for j in range(HALF):
                hit = node == local[j : j + 1]
                for c in range(2):
                    sums[c] = sums[c] + jnp.where(hit, values[c][j : j + 1], 0.0)
    ones = jnp.ones((8, SIDE), f32)
    for c in range(2):
        summed = lax.dot_general(
            ones,
            sums[c],
            (((1,), (1,)), ((), ())),
            precision=lax.Precision.HIGHEST,
            preferred_element_type=f32,
        )
        out_ref[c : c + 1] = summed[0:1]


def collect(packed):
    return pl.pallas_call(
        collect_kernel,
        out_shape=jax.ShapeDtypeStruct((2, SIDE), f32),
        in_specs=[pl.BlockSpec(memory_space=pltpu.VMEM)],
        out_specs=pl.BlockSpec(memory_space=pltpu.VMEM),
        compiler_params=pltpu.CompilerParams(vmem_limit_bytes=8 * 1024 * 1024),
    )(packed)


def swap(x, bit):
    pairs = [(i, i ^ (1 << bit)) for i in range(lax.axis_size("tiles"))]
    return lax.ppermute(x, "tiles", pairs)


def on_device(strips, edge_colour, patch_offsets, patch_live, node_ids):
    tables = [jnp.asarray(table) for table in fourier_tables()]
    corners = jnp.transpose(patch_offsets, (0, 1, 3, 2))
    held, send_early = hold(edge_colour, corners, strips)
    far_early = swap(send_early, BITS[0])
    far_late = swap(cut_late(edge_colour, corners, held), BITS[1])
    near_early, near_late = near_spectra(edge_colour, corners, held, *tables)
    early = correlate_early(near_early, far_early, tables)
    packed = correlate_late(patch_live, node_ids, early, near_late, far_late, tables)
    packed = packed.reshape(SIDE, 1, SIDE)
    gathered = lax.all_to_all(packed, ("tiles", "grp"), 0, 0, tiled=True)
    return collect(gathered.reshape(SIDE, SIDE))


def solution(mesh):
    placed = (
        P(("tiles", "grp"), None, None),
        P(("tiles", "grp"), None),
        P(("tiles", "grp"), None, None, None),
        P(("tiles", "grp"), None),
        P(("tiles", "grp"), None, None),
    )
    return jax.shard_map(
        on_device, mesh=mesh, in_specs=placed, out_specs=P(None, ("tiles", "grp")), check_vma=False
    )
```

time: 43.1 us -> 40 us (0.928)
  local copies, waits for them, and re-layouts: 1.36 us -> 0.03 us
  Pallas kernels: 14.1 us -> 13 us
  blocking collectives: 20.9 us -> 20 us
    unnamed x14 -> x12, local copies, waits for them, and re-layouts: 1.36 us -> 0.03 us
    pallas_call x1, Pallas kernels: 2.27 us -> 1.43 us  [collect(): pl.pallas_call(collect_kernel, out_shape=jax.ShapeDtypeStruct((2, SIDE),...]
    all_to_all x1, blocking collectives: 20.9 us -> 20 us  [on_device(): gathered = lax.all_to_all(packed, ('tiles', 'grp'), 0, 0, tiled=True)]
    pallas_call x3 -> x4, Pallas kernels: 8.15 us -> 8.19 us  [the longest x1 2.57 us: hold(): pl.pallas_call(hold_kernel, out_shape=(jax.ShapeDtypeStruct(strips.shape,...]
  transfers between devices with their start and end apart: 2 -> 2, of which waited for: 1 -> 1; matrix products, arithmetic and copies ran while one was open for 0% -> 0% of each run, Pallas kernels for 11% -> 14%
where the time goes in v3:
time: 40 us; the launch traced here: 39.9 us
  blocking collectives  20 us (50%)
  Pallas kernels  13 us (32%)
  starting transfers between devices  5.8 us (14%)
  waiting for transfers between devices  0.94 us (2%)
    all_to_all x1, blocking collectives, on_device(): gathered = lax.all_to_all(packed, ('tiles', 'grp'), 0, 0, tiled=True)  20 us
    ppermute x2, starting transfers between devices, swap(): return lax.ppermute(x, 'tiles', pairs)  5.8 us
    pallas_call x1, Pallas kernels, correlate_late(): pl.pallas_call(late_kernel, out_shape=jax.ShapeDtypeStruct((SIDE, SIDE),...  3.37 us
    pallas_call x1, Pallas kernels, hold(): pl.pallas_call(hold_kernel, out_shape=(jax.ShapeDtypeStruct(strips.shape,...  2.57 us
    pallas_call x1, Pallas kernels, correlate_early(): pl.pallas_call(correlate_group, out_shape=jax.ShapeDtypeStruct((3, HALF,...  2.57 us
    pallas_call x1, Pallas kernels, near_spectra(): pl.pallas_call(near_kernel, out_shape=(shape, shape), in_specs=[scalars,...  2.19 us
    pallas_call x1, Pallas kernels, collect(): pl.pallas_call(collect_kernel, out_shape=jax.ShapeDtypeStruct((2, SIDE),...  1.43 us
    ppermute x2, waiting for transfers between devices, swap(): return lax.ppermute(x, 'tiles', pairs)  0.94 us
  transfers between devices with their start and end apart: 2, of which 1 were waited for; matrix products, arithmetic and copies ran while one was open for 0% of the time, Pallas kernels for 14%

profile of v3, /device:TPU:1, one launch (start us, length us, event | category | flops | bytes accessed | tf_op | source)
XLA Modules:
  0.0 39.9 jit_solution(13363404284262481157)
XLA Ops:
  0.0 0.0 copy-start.3
  0.0 0.0 copy-start.2
  0.0 0.0 copy-start
  0.0 0.0 copy-start.1
  0.0 2.6 %shard_map.73 = (bf16[2,256,4096]{2,1,0:T(8,128)(2,1)S(1)}, bf16[8,128,128]{2,1,0:T(8,128)(2,1)S(1)}) custom-call(s32[1,2]{1,0:T(1,128)} %colour_ref.3, s32[1,2,2,16]{3,2,1,0:T(2,128)} %bitcast.7, bf16[2,256,4096]{2,1,0:T(8,128)(2,1)} %strips_ref.1), custom_call_target="tpu_custom_call" | custom-call | flops 1048576 | bytes 4194304 | tf_op jit(solution)/shard_map/pallas_call | solution.py:107
  2.6 2.1 %collective-permute-start = (bf16[8,128,128]{2,1,0:T(8,128)(2,1)S(1)}, bf16[8,128,128]{2,1,0:T(8,128)(2,1)S(1)}, u32[]{:S(2)}, u32[]{:S(2)}) collective-permute-start(bf16[8,128,128]{2,1,0:T(8,128)(2,1)S(1)} %get-tuple-element.11), channel_id=1, source_target_pairs={{0,2},{2,0},{4,6},{6,4},{8,10},{10,8},{12,14},{14,12},{16,18},{18,... | collective-permute-start | bytes 786440 | tf_op jit(solution)/shard_map/ppermute | solution.py:357
  4.7 0.0 copy-done.3
  4.7 0.0 copy-done.2
  4.7 0.9 %shard_map.76 = bf16[8,128,128]{2,1,0:T(8,128)(2,1)S(1)} custom-call(s32[1,2]{1,0:T(1,128)S(1)} %copy-done.3, s32[1,2,2,16]{3,2,1,0:T(2,128)S(1)} %bitcast.8, bf16[2,256,4096]{2,1,0:T(8,128)(2,1)S(1)} %get-tuple-element.9.held_ref), custom_call_target="tpu_custom_call" | custom-call | flops 1048576 | bytes 262144 | tf_op jit(solution)/shard_map/pallas_call | solution.py:127
  5.6 0.0 copy-start.4
  5.6 0.0 copy-start.5
  5.6 3.7 %collective-permute-start.1 = (bf16[8,128,128]{2,1,0:T(8,128)(2,1)S(1)}, bf16[8,128,128]{2,1,0:T(8,128)(2,1)S(1)}, u32[]{:S(2)}, u32[]{:S(2)}) collective-permute-start(bf16[8,128,128]{2,1,0:T(8,128)(2,1)S(1)} %shard_map.76), channel_id=1, source_target_pairs={{0,64},{2,66},{4,68},{6,70},{8,72},{10,74},{12,76},{14,78},{16,80}... | collective-permute-start | bytes 786440 | tf_op jit(solution)/shard_map/ppermute | solution.py:357
  9.3 0.0 copy-done
  9.3 0.0 copy-done.1
  9.3 2.2 %shard_map.74 = (f32[1024,256]{1,0:T(8,128)S(1)}, f32[1024,256]{1,0:T(8,128)S(1)}) custom-call(s32[1,2]{1,0:T(1,128)S(1)} %copy-done.3, s32[1,2,2,16]{3,2,1,0:T(2,128)S(1)} %bitcast.9, bf16[2,256,4096]{2,1,0:T(8,128)(2,1)S(1)} %get-tuple-element.9.held_ref, bf16[256,256]{1,0:T(8,128)(2,1)S(1)} %copy-done.1, bf16[768,256]{1,0:T(8,128)(2,1)S(1)} %copy-done), custom_call_target="tpu_custom_call" | custom-call | flops 1073741824 | bytes 2621440 | tf_op jit(solution)/shard_map/pallas_call | solution.py:174
  11.5 0.0 collective-permute-done.window_ref
  11.5 2.6 %shard_map.75.early_ref = f32[3,8,128]{2,1,0:T(8,128)S(1)} custom-call(f32[1024,256]{1,0:T(8,128)S(1)} %get-tuple-element.10.near_ref, bf16[8,128,128]{2,1,0:T(8,128)(2,1)S(1)} %collective-permute-done.window_ref, bf16[256,256]{1,0:T(8,128)(2,1)S(1)} %copy-done.1, bf16[768,256]{1,0:T(8,128)(2,1)S(1)} %copy-done), custom_call_target="tpu_custom_call" | custom-call | flops 805306368 | bytes 1310720 | tf_op jit(solution)/shard_map/pallas_call | solution.py:283
  14.1 0.9 %collective-permute-done.1.window_ref = bf16[8,128,128]{2,1,0:T(8,128)(2,1)S(1)} collective-permute-done((bf16[8,128,128]{2,1,0:T(8,128)(2,1)S(1)}, bf16[8,128,128]{2,1,0:T(8,128)(2,1)S(1)}, u32[]{:S(2)}, u32[]{:S(2)}) %collective-permute-start.1) | collective-permute-done | bytes 262176 | tf_op jit(solution)/shard_map/ppermute | solution.py:357
  15.0 0.0 copy-done.4
  15.0 0.0 copy-done.5
  15.0 3.4 %shard_map.77 = f32[128,128]{1,0:T(8,128)S(1)} custom-call(s32[1,2]{1,0:T(1,128)S(1)} %copy-done.5, s32[1,2,16]{2,1,0:T(2,128)S(1)} %copy-done.4, f32[3,8,128]{2,1,0:T(8,128)S(1)} %shard_map.75.early_ref, f32[1024,256]{1,0:T(8,128)S(1)} %get-tuple-element.12.near_ref, bf16[8,128,128]{2,1,0:T(8,128)(2,1)S(1)} %collective-permute-done.1.window_ref, ...), custom_call_target="tpu_custom_call" | custom-call | flops 805306368 | bytes 1310720 | tf_op jit(solution)/shard_map/pallas_call | solution.py:294
  18.4 20.0 %all_to_all.5 = f32[128,1,128]{2,1,0:T(1,128)S(1)} all-to-all(f32[128,1,128]{2,1,0:T(1,128)S(1)} %bitcast.6), channel_id=1, replica_groups=mesh['tiles'=64,'grp'=2] {'tiles','grp'}, dimensions={0} | all-to-all | bytes 131072 | tf_op jit(solution)/shard_map/all_to_all | solution.py:370
  38.4 1.4 %shard_map.78 = f32[2,128]{1,0:T(2,128)} custom-call(f32[128,128]{1,0:T(8,128)S(1)} %bitcast.5), custom_call_target="tpu_custom_call" | custom-call | tf_op jit(solution)/shard_map/pallas_call | solution.py:346
Async XLA Ops:
  0.0 4.7 %copy-start.3 = (s32[1,2]{1,0:T(1,128)S(1)}, s32[1,2]{1,0:T(1,128)}, u32[]{:S(2)}) copy-start(s32[1,2]{1,0:T(1,128)} %colour_ref.3) | copy-start | bytes 28
  0.0 4.7 %copy-start.2 = (s32[1,2,16,2]{2,3,1,0:T(2,128)S(1)}, s32[1,2,16,2]{2,3,1,0:T(2,128)}, u32[]{:S(2)}) copy-start(s32[1,2,16,2]{2,3,1,0:T(2,128)} %param.9) | copy-start | bytes 772
  0.0 9.3 %copy-start = (bf16[768,256]{1,0:T(8,128)(2,1)S(1)}, bf16[768,256]{1,0:T(8,128)(2,1)}, u32[]{:S(2)}) copy-start(bf16[768,256]{1,0:T(8,128)(2,1)} %constant.5.clone.second_ref) | copy-start | bytes 1179652
  0.0 9.3 %copy-start.1 = (bf16[256,256]{1,0:T(8,128)(2,1)S(1)}, bf16[256,256]{1,0:T(8,128)(2,1)}, u32[]{:S(2)}) copy-start(bf16[256,256]{1,0:T(8,128)(2,1)} %constant.4.clone.first_ref) | copy-start | bytes 393220
  2.6 8.9 %collective-permute-start = (bf16[8,128,128]{2,1,0:T(8,128)(2,1)S(1)}, bf16[8,128,128]{2,1,0:T(8,128)(2,1)S(1)}, u32[]{:S(2)}, u32[]{:S(2)}) collective-permute-start(bf16[8,128,128]{2,1,0:T(8,128)(2,1)S(1)} %get-tuple-element.11), channel_id=1, source_target_pairs={{0,2},{2,0},{4,6},{6,4},{8,10},{10,8},{12,14},{14,12},{16,18},{18,... | collective-permute-start | bytes 786440 | tf_op jit(solution)/shard_map/ppermute | solution.py:357
  5.6 9.4 %copy-start.4 = (s32[1,2,16]{2,1,0:T(2,128)S(1)}, s32[1,2,16]{2,1,0:T(2,128)}, u32[]{:S(2)}) copy-start(s32[1,2,16]{2,1,0:T(2,128)} %ids_ref.1) | copy-start | bytes 388
  5.6 9.4 %copy-start.5 = (s32[1,2]{1,0:T(1,128)S(1)}, s32[1,2]{1,0:T(1,128)}, u32[]{:S(2)}) copy-start(s32[1,2]{1,0:T(1,128)} %live_ref.1) | copy-start | bytes 28
  5.6 9.4 %collective-permute-start.1 = (bf16[8,128,128]{2,1,0:T(8,128)(2,1)S(1)}, bf16[8,128,128]{2,1,0:T(8,128)(2,1)S(1)}, u32[]{:S(2)}, u32[]{:S(2)}) collective-permute-start(bf16[8,128,128]{2,1,0:T(8,128)(2,1)S(1)} %shard_map.76), channel_id=1, source_target_pairs={{0,64},{2,66},{4,68},{6,70},{8,72},{10,74},{12,76},{14,78},{16,80}... | collective-permute-start | bytes 786440 | tf_op jit(solution)/shard_map/ppermute | solution.py:357

commit v4 on v3

--- a/solution.py
+++ b/solution.py
@@ -66,7 +66,16 @@
 
 
 def hold_kernel(
-    colour_hbm, corner_hbm, strips_ref, held_ref, send_ref, colour_ref, corner_ref, sems, small_sems
+    colour_hbm,
+    corner_hbm,
+    strips_ref,
+    held_ref,
+    early_ref,
+    late_ref,
+    colour_ref,
+    corner_ref,
+    sems,
+    small_sems,
 ):
     small = [
         pltpu.make_async_copy(colour_hbm, colour_ref, small_sems.at[0]),
@@ -83,13 +92,9 @@
         copy.start()
     for copy in small + large:
         copy.wait()
-    for j, window in enumerate(cut_windows(0, False, colour_ref, corner_ref, held_ref)):
-        send_ref[j] = window
-
-
-def send_kernel(colour_ref, corner_ref, held_ref, send_ref):
-    for j, window in enumerate(cut_windows(1, False, colour_ref, corner_ref, held_ref)):
-        send_ref[j] = window
+    for r, send_ref in enumerate((early_ref, late_ref)):
+        for j, window in enumerate(cut_windows(r, False, colour_ref, corner_ref, held_ref)):
+            send_ref[j] = window
 
 
 scalars = pl.BlockSpec(memory_space=pltpu.SMEM)
@@ -109,9 +114,10 @@
         out_shape=(
             jax.ShapeDtypeStruct(strips.shape, bf16),
             jax.ShapeDtypeStruct((HALF, SIDE, SIDE), bf16),
+            jax.ShapeDtypeStruct((HALF, SIDE, SIDE), bf16),
         ),
         in_specs=[far_memory] * 3,
-        out_specs=(vectors, vectors),
+        out_specs=(vectors,) * 3,
         scratch_shapes=[
             pltpu.SMEM(colour.shape, jnp.int32),
             pltpu.SMEM(corners.shape, jnp.int32),
@@ -121,17 +127,6 @@
         compiler_params=pltpu.CompilerParams(vmem_limit_bytes=16 * 1024 * 1024),
         cost_estimate=cut_cost(2 * strips.size),
     )(*(pltpu.with_memory_space_constraint(x, pltpu.HBM) for x in (colour, corners, strips)))
-
-
-def cut_late(colour, corners, held):
-    return pl.pallas_call(
-        send_kernel,
-        out_shape=jax.ShapeDtypeStruct((HALF, SIDE, SIDE), bf16),
-        in_specs=[scalars, scalars, vectors],
-        out_specs=vectors,
-        compiler_params=pltpu.CompilerParams(vmem_limit_bytes=16 * 1024 * 1024),
-        cost_estimate=cut_cost(HALF * CELLS * 2),
-    )(colour, corners, held)
 
 
 def split(x):
@@ -246,27 +241,21 @@
     live_ref, ids_ref, early_ref, near_ref, window_ref, first_ref, second_ref, out_ref, late_ref
 ):
     correlate_group(near_ref, window_ref, first_ref, second_ref, late_ref)
-    lane = lax.broadcasted_iota(jnp.int32, (8, SIDE), 1)
-    sublane = lax.broadcasted_iota(jnp.int32, (8, SIDE), 0)
-    coord = (((lane + SIDE // 2) & (SIDE - 1)) - SIDE // 2).astype(f32)
-    chosen = jnp.where(lane == SIDE // 2, 1.0, 0.0)
-    query = jnp.where(sublane == 0, 1.0, jnp.where(sublane == 1, coord, chosen))
     terms = []
     for i in range(3):
         terms += [early_ref[i], late_ref[i]]
-    sums = lax.dot_general(
-        query,
-        jnp.concatenate(terms, axis=0),
-        (((1,), (1,)), ((), ())),
-        precision=lax.Precision.HIGHEST,
-        preferred_element_type=f32,
-    )
+    terms.append(jnp.zeros((SIDE - 3 * SLOTS, SIDE), f32))
+    flat = jnp.concatenate(terms, axis=0).T
+    index = lax.broadcasted_iota(jnp.int32, (SIDE, SIDE), 0)
+    coord = (((index + SIDE // 2) & (SIDE - 1)) - SIDE // 2).astype(f32)
+    sums = down(flat)
+    ramped = down(flat * coord)
     slot = lax.broadcasted_iota(jnp.int32, (1, SLOTS), 1)
     pieces = []
     for r in range(2):
         ids = jnp.where(slot < live_ref[0, r], ids_ref[0, r : r + 1, :], -1)
         pieces.append(ids.astype(f32))
-    pieces += [sums[0:1], sums[1:2, :SLOTS], sums[2:3, :SLOTS]]
+    pieces += [sums[:, : 3 * SLOTS], ramped[:, :SLOTS], flat[SIDE // 2 : SIDE // 2 + 1, :SLOTS]]
     pieces.append(jnp.zeros((1, SIDE - 7 * SLOTS), f32))
     out_ref[...] = jnp.broadcast_to(jnp.concatenate(pieces, axis=1), (SIDE, SIDE))
 
@@ -330,16 +319,8 @@
                 hit = node == local[j : j + 1]
                 for c in range(2):
                     sums[c] = sums[c] + jnp.where(hit, values[c][j : j + 1], 0.0)
-    ones = jnp.ones((8, SIDE), f32)
     for c in range(2):
-        summed = lax.dot_general(
-            ones,
-            sums[c],
-            (((1,), (1,)), ((), ())),
-            precision=lax.Precision.HIGHEST,
-            preferred_element_type=f32,
-        )
-        out_ref[c : c + 1] = summed[0:1]
+        out_ref[c : c + 1] = down(sums[c].T)
 
 
 def collect(packed):
@@ -360,9 +341,9 @@
 def on_device(strips, edge_colour, patch_offsets, patch_live, node_ids):
     tables = [jnp.asarray(table) for table in fourier_tables()]
     corners = jnp.transpose(patch_offsets, (0, 1, 3, 2))
-    held, send_early = hold(edge_colour, corners, strips)
+    held, send_early, send_late = hold(edge_colour, corners, strips)
     far_early = swap(send_early, BITS[0])
-    far_late = swap(cut_late(edge_colour, corners, held), BITS[1])
+    far_late = swap(send_late, BITS[1])
     near_early, near_late = near_spectra(edge_colour, corners, held, *tables)
     early = correlate_early(near_early, far_early, tables)
     packed = correlate_late(patch_live, node_ids, early, near_late, far_late, tables)

time: 40 us -> 39.2 us (0.980)
  Pallas kernels: 13 us -> 12.1 us
    pallas_call x1 -> x0, Pallas kernels: 0.86 us -> none  [cut_late(): pl.pallas_call(send_kernel, out_shape=jax.ShapeDtypeStruct((HALF, SIDE, S...]
  transfers between devices with their start and end apart: 2 -> 2, of which waited for: 1 -> 1; matrix products, arithmetic and copies ran while one was open for 0% -> 0% of each run, Pallas kernels for 14% -> 12%
where the time goes in v4:
time: 39.2 us; the launch traced here: 39 us
  blocking collectives  20.2 us (52%)
  Pallas kernels  12.1 us (31%)
  starting transfers between devices  5.72 us (15%)
  waiting for transfers between devices  0.93 us (2%)
    all_to_all x1, blocking collectives, on_device(): gathered = lax.all_to_all(packed, ('tiles', 'grp'), 0, 0, tiled=True)  20.2 us
    ppermute x2, starting transfers between devices, swap(): return lax.ppermute(x, 'tiles', pairs)  5.72 us
    pallas_call x1, Pallas kernels, correlate_late(): pl.pallas_call(late_kernel, out_shape=jax.ShapeDtypeStruct((SIDE, SIDE),...  3.3 us
    pallas_call x1, Pallas kernels, hold(): pl.pallas_call(hold_kernel, out_shape=(jax.ShapeDtypeStruct(strips.shape,...  2.84 us
    pallas_call x1, Pallas kernels, correlate_early(): pl.pallas_call(correlate_group, out_shape=jax.ShapeDtypeStruct((3, HALF,...  2.57 us
    pallas_call x1, Pallas kernels, near_spectra(): pl.pallas_call(near_kernel, out_shape=(shape, shape), in_specs=[scalars,...  2.19 us
    pallas_call x1, Pallas kernels, collect(): pl.pallas_call(collect_kernel, out_shape=jax.ShapeDtypeStruct((2, SIDE),...  1.2 us
    ppermute x2, waiting for transfers between devices, swap(): return lax.ppermute(x, 'tiles', pairs)  0.93 us
  transfers between devices with their start and end apart: 2, of which 1 were waited for; matrix products, arithmetic and copies ran while one was open for 0% of the time, Pallas kernels for 12%

profile of v4, /device:TPU:1, one launch (start us, length us, event | category | flops | bytes accessed | tf_op | source)
XLA Modules:
  0.0 39.0 jit_solution(17939025712796769032)
XLA Ops:
  0.0 0.0 copy-start
  0.0 0.0 copy-start.1
  0.0 0.0 copy-start.3
  0.0 0.0 copy-start.2
  0.0 2.8 %shard_map.73 = (bf16[2,256,4096]{2,1,0:T(8,128)(2,1)S(1)}, bf16[8,128,128]{2,1,0:T(8,128)(2,1)S(1)}, bf16[8,128,128]{2,1,0:T(8,128)(2,1)S(1)}) custom-call(s32[1,2]{1,0:T(1,128)} %colour_ref.1, s32[1,2,2,16]{3,2,1,0:T(2,128)} %bitcast.7, bf16[2,256,4096]{2,1,0:T(8,128)(2,1)} %strips_ref.1), custom_call_target="tpu_custom_call" | custom-call | flops 1048576 | bytes 4194304 | tf_op jit(solution)/shard_map/pallas_call | solution.py:112
  2.9 0.0 copy-start.4
  2.9 0.0 copy-start.5
  2.9 2.1 %collective-permute-start = (bf16[8,128,128]{2,1,0:T(8,128)(2,1)S(1)}, bf16[8,128,128]{2,1,0:T(8,128)(2,1)S(1)}, u32[]{:S(2)}, u32[]{:S(2)}) collective-permute-start(bf16[8,128,128]{2,1,0:T(8,128)(2,1)S(1)} %get-tuple-element.12), channel_id=1, source_target_pairs={{0,2},{2,0},{4,6},{6,4},{8,10},{10,8},{12,14},{14,12},{16,18},{18,... | collective-permute-start | bytes 786440 | tf_op jit(solution)/shard_map/ppermute | solution.py:338
  5.0 3.6 %collective-permute-start.1 = (bf16[8,128,128]{2,1,0:T(8,128)(2,1)S(1)}, bf16[8,128,128]{2,1,0:T(8,128)(2,1)S(1)}, u32[]{:S(2)}, u32[]{:S(2)}) collective-permute-start(bf16[8,128,128]{2,1,0:T(8,128)(2,1)S(1)} %get-tuple-element.14), channel_id=1, source_target_pairs={{0,64},{2,66},{4,68},{6,70},{8,72},{10,74},{12,76},{14,78},{16,80}... | collective-permute-start | bytes 786440 | tf_op jit(solution)/shard_map/ppermute | solution.py:338
  8.6 0.0 copy-done
  8.6 0.0 copy-done.1
  8.6 0.0 copy-done.3
  8.6 0.0 copy-done.2
  8.6 2.2 %shard_map.74 = (f32[1024,256]{1,0:T(8,128)S(1)}, f32[1024,256]{1,0:T(8,128)S(1)}) custom-call(s32[1,2]{1,0:T(1,128)S(1)} %copy-done.3, s32[1,2,2,16]{3,2,1,0:T(2,128)S(1)} %bitcast.8, bf16[2,256,4096]{2,1,0:T(8,128)(2,1)S(1)} %get-tuple-element.10.held_ref, bf16[256,256]{1,0:T(8,128)(2,1)S(1)} %copy-done.1, bf16[768,256]{1,0:T(8,128)(2,1)S(1)} %copy-done), custom_call_target="tpu_custom_call" | custom-call | flops 1073741824 | bytes 2621440 | tf_op jit(solution)/shard_map/pallas_call | solution.py:169
  10.8 0.0 collective-permute-done.window_ref
  10.8 2.6 %shard_map.75.early_ref = f32[3,8,128]{2,1,0:T(8,128)S(1)} custom-call(f32[1024,256]{1,0:T(8,128)S(1)} %get-tuple-element.11.near_ref, bf16[8,128,128]{2,1,0:T(8,128)(2,1)S(1)} %collective-permute-done.window_ref, bf16[256,256]{1,0:T(8,128)(2,1)S(1)} %copy-done.1, bf16[768,256]{1,0:T(8,128)(2,1)S(1)} %copy-done), custom_call_target="tpu_custom_call" | custom-call | flops 805306368 | bytes 1310720 | tf_op jit(solution)/shard_map/pallas_call | solution.py:272
  13.4 0.9 %collective-permute-done.1.window_ref = bf16[8,128,128]{2,1,0:T(8,128)(2,1)S(1)} collective-permute-done((bf16[8,128,128]{2,1,0:T(8,128)(2,1)S(1)}, bf16[8,128,128]{2,1,0:T(8,128)(2,1)S(1)}, u32[]{:S(2)}, u32[]{:S(2)}) %collective-permute-start.1) | collective-permute-done | bytes 262176 | tf_op jit(solution)/shard_map/ppermute | solution.py:338
  14.3 0.0 copy-done.4
  14.3 0.0 copy-done.5
  14.3 3.3 %shard_map.76 = f32[128,128]{1,0:T(8,128)S(1)} custom-call(s32[1,2]{1,0:T(1,128)S(1)} %copy-done.5, s32[1,2,16]{2,1,0:T(2,128)S(1)} %copy-done.4, f32[3,8,128]{2,1,0:T(8,128)S(1)} %shard_map.75.early_ref, f32[1024,256]{1,0:T(8,128)S(1)} %get-tuple-element.13.near_ref, bf16[8,128,128]{2,1,0:T(8,128)(2,1)S(1)} %collective-permute-done.1.window_ref, ...), custom_call_target="tpu_custom_call" | custom-call | flops 805306368 | bytes 1310720 | tf_op jit(solution)/shard_map/pallas_call | solution.py:283
  17.6 20.2 %all_to_all.5 = f32[128,1,128]{2,1,0:T(1,128)S(1)} all-to-all(f32[128,1,128]{2,1,0:T(1,128)S(1)} %bitcast.6), channel_id=1, replica_groups=mesh['tiles'=64,'grp'=2] {'tiles','grp'}, dimensions={0} | all-to-all | bytes 131072 | tf_op jit(solution)/shard_map/all_to_all | solution.py:351
  37.8 1.2 %shard_map.77 = f32[2,128]{1,0:T(2,128)} custom-call(f32[128,128]{1,0:T(8,128)S(1)} %bitcast.5), custom_call_target="tpu_custom_call" | custom-call | tf_op jit(solution)/shard_map/pallas_call | solution.py:327
Async XLA Ops:
  0.0 8.6 %copy-start = (bf16[768,256]{1,0:T(8,128)(2,1)S(1)}, bf16[768,256]{1,0:T(8,128)(2,1)}, u32[]{:S(2)}) copy-start(bf16[768,256]{1,0:T(8,128)(2,1)} %constant.5.clone.second_ref) | copy-start | bytes 1179652
  0.0 8.6 %copy-start.1 = (bf16[256,256]{1,0:T(8,128)(2,1)S(1)}, bf16[256,256]{1,0:T(8,128)(2,1)}, u32[]{:S(2)}) copy-start(bf16[256,256]{1,0:T(8,128)(2,1)} %constant.4.clone.first_ref) | copy-start | bytes 393220
  0.0 8.6 %copy-start.3 = (s32[1,2]{1,0:T(1,128)S(1)}, s32[1,2]{1,0:T(1,128)}, u32[]{:S(2)}) copy-start(s32[1,2]{1,0:T(1,128)} %colour_ref.1) | copy-start | bytes 28
  0.0 8.6 %copy-start.2 = (s32[1,2,16,2]{2,3,1,0:T(2,128)S(1)}, s32[1,2,16,2]{2,3,1,0:T(2,128)}, u32[]{:S(2)}) copy-start(s32[1,2,16,2]{2,3,1,0:T(2,128)} %param.9) | copy-start | bytes 772
  2.9 11.5 %copy-start.4 = (s32[1,2,16]{2,1,0:T(2,128)S(1)}, s32[1,2,16]{2,1,0:T(2,128)}, u32[]{:S(2)}) copy-start(s32[1,2,16]{2,1,0:T(2,128)} %ids_ref.1) | copy-start | bytes 388
  2.9 11.4 %copy-start.5 = (s32[1,2]{1,0:T(1,128)S(1)}, s32[1,2]{1,0:T(1,128)}, u32[]{:S(2)}) copy-start(s32[1,2]{1,0:T(1,128)} %live_ref.1) | copy-start | bytes 28
  2.9 7.9 %collective-permute-start = (bf16[8,128,128]{2,1,0:T(8,128)(2,1)S(1)}, bf16[8,128,128]{2,1,0:T(8,128)(2,1)S(1)}, u32[]{:S(2)}, u32[]{:S(2)}) collective-permute-start(bf16[8,128,128]{2,1,0:T(8,128)(2,1)S(1)} %get-tuple-element.12), channel_id=1, source_target_pairs={{0,2},{2,0},{4,6},{6,4},{8,10},{10,8},{12,14},{14,12},{16,18},{18,... | collective-permute-start | bytes 786440 | tf_op jit(solution)/shard_map/ppermute | solution.py:338
  5.0 9.3 %collective-permute-start.1 = (bf16[8,128,128]{2,1,0:T(8,128)(2,1)S(1)}, bf16[8,128,128]{2,1,0:T(8,128)(2,1)S(1)}, u32[]{:S(2)}, u32[]{:S(2)}) collective-permute-start(bf16[8,128,128]{2,1,0:T(8,128)(2,1)S(1)} %get-tuple-element.14), channel_id=1, source_target_pairs={{0,64},{2,66},{4,68},{6,70},{8,72},{10,74},{12,76},{14,78},{16,80}... | collective-permute-start | bytes 786440 | tf_op jit(solution)/shard_map/ppermute | solution.py:338

commit v5 on v4

--- a/solution.py
+++ b/solution.py
@@ -204,10 +204,17 @@
         sizes.append(size)
         size_rows.append(down(size))
     floors = across(size_rows) * (0.1 / CELLS) + 1e-6
-    whites = []
+    whites, power_rows, centres = [], [], []
     for p in range(HALF):
         scale = 1.0 / (sizes[p] + floors[p : p + 1])
-        whites.append((crosses[p][0] * scale, crosses[p][1] * scale))
+        white = (crosses[p][0] * scale, crosses[p][1] * scale)
+        whites.append(white)
+        weighted = sizes[p] * scale
+        power_rows.append(down(weighted * weighted))
+        centres.append(white[0][0:1, 0:1])
+    centre = jnp.concatenate(centres, axis=0)
+    variance = jnp.maximum(across(power_rows) - centre * centre, 0.0)
+    factor = (2.0 / CELLS) / jnp.sqrt(variance * (1.0 / CELLS**2) + 1e-6)
     spectra = []
     for q in range(HALF // 2):
         (a_real, a_imag), (b_real, b_imag) = whites[2 * q], whites[2 * q + 1]
@@ -219,15 +226,11 @@
     for p in range(HALF):
         q, h = divmod(p, 2)
         patches.append(patch_rows(surfaces, q)[:, h * SIDE : (h + 1) * SIDE])
-    mean = across([down(x) for x in patches]) * (1.0 / CELLS)
-    square = across([down(x * x) for x in patches]) * (1.0 / CELLS)
     peak = jnp.max(
         jnp.concatenate([jnp.max(x, axis=0, keepdims=True) for x in patches], axis=0),
         axis=1,
         keepdims=True,
     )
-    variance = jnp.maximum(square - mean * mean, 0.0)
-    factor = (2.0 / CELLS) / jnp.sqrt(variance * (1.0 / CELLS**2) + 1e-6)
     row_index = lax.broadcasted_iota(jnp.int32, (SIDE, SIDE), 0)
     row_coord = (((row_index + SIDE // 2) & (SIDE - 1)) - SIDE // 2).astype(f32)
     for p, surface in enumerate(patches):

time: 39.2 us -> 39.1 us (level)
  no operation moved by 1% of the time
where the time goes in v5:
time: 39.1 us; the launch traced here: 39 us
  blocking collectives  20.2 us (52%)
  Pallas kernels  12.1 us (31%)
  starting transfers between devices  5.72 us (15%)
  waiting for transfers between devices  0.93 us (2%)
    all_to_all x1, blocking collectives, on_device(): gathered = lax.all_to_all(packed, ('tiles', 'grp'), 0, 0, tiled=True)  20.2 us
    ppermute x2, starting transfers between devices, swap(): return lax.ppermute(x, 'tiles', pairs)  5.72 us
    pallas_call x1, Pallas kernels, correlate_late(): pl.pallas_call(late_kernel, out_shape=jax.ShapeDtypeStruct((SIDE, SIDE),...  3.29 us
    pallas_call x1, Pallas kernels, hold(): pl.pallas_call(hold_kernel, out_shape=(jax.ShapeDtypeStruct(strips.shape,...  2.84 us
    pallas_call x1, Pallas kernels, correlate_early(): pl.pallas_call(correlate_group, out_shape=jax.ShapeDtypeStruct((3, HALF,...  2.56 us
    pallas_call x1, Pallas kernels, near_spectra(): pl.pallas_call(near_kernel, out_shape=(shape, shape), in_specs=[scalars,...  2.19 us
    pallas_call x1, Pallas kernels, collect(): pl.pallas_call(collect_kernel, out_shape=jax.ShapeDtypeStruct((2, SIDE),...  1.2 us
    ppermute x2, waiting for transfers between devices, swap(): return lax.ppermute(x, 'tiles', pairs)  0.93 us
  transfers between devices with their start and end apart: 2, of which 1 were waited for; matrix products, arithmetic and copies ran while one was open for 0% of the time, Pallas kernels for 12%

profile of v5, /device:TPU:1, one launch (start us, length us, event | category | flops | bytes accessed | tf_op | source)
XLA Modules:
  0.0 39.0 jit_solution(8616009508722788230)
XLA Ops:
  0.0 0.0 copy-start
  0.0 0.0 copy-start.1
  0.0 0.0 copy-start.3
  0.0 0.0 copy-start.2
  0.0 2.8 %shard_map.73 = (bf16[2,256,4096]{2,1,0:T(8,128)(2,1)S(1)}, bf16[8,128,128]{2,1,0:T(8,128)(2,1)S(1)}, bf16[8,128,128]{2,1,0:T(8,128)(2,1)S(1)}) custom-call(s32[1,2]{1,0:T(1,128)} %colour_ref.1, s32[1,2,2,16]{3,2,1,0:T(2,128)} %bitcast.7, bf16[2,256,4096]{2,1,0:T(8,128)(2,1)} %strips_ref.1), custom_call_target="tpu_custom_call" | custom-call | flops 1048576 | bytes 4194304 | tf_op jit(solution)/shard_map/pallas_call | solution.py:112
  2.9 0.0 copy-start.4
  2.9 0.0 copy-start.5
  2.9 2.1 %collective-permute-start = (bf16[8,128,128]{2,1,0:T(8,128)(2,1)S(1)}, bf16[8,128,128]{2,1,0:T(8,128)(2,1)S(1)}, u32[]{:S(2)}, u32[]{:S(2)}) collective-permute-start(bf16[8,128,128]{2,1,0:T(8,128)(2,1)S(1)} %get-tuple-element.12), channel_id=1, source_target_pairs={{0,2},{2,0},{4,6},{6,4},{8,10},{10,8},{12,14},{14,12},{16,18},{18,... | collective-permute-start | bytes 786440 | tf_op jit(solution)/shard_map/ppermute | solution.py:341
  5.0 3.6 %collective-permute-start.1 = (bf16[8,128,128]{2,1,0:T(8,128)(2,1)S(1)}, bf16[8,128,128]{2,1,0:T(8,128)(2,1)S(1)}, u32[]{:S(2)}, u32[]{:S(2)}) collective-permute-start(bf16[8,128,128]{2,1,0:T(8,128)(2,1)S(1)} %get-tuple-element.14), channel_id=1, source_target_pairs={{0,64},{2,66},{4,68},{6,70},{8,72},{10,74},{12,76},{14,78},{16,80}... | collective-permute-start | bytes 786440 | tf_op jit(solution)/shard_map/ppermute | solution.py:341
  8.6 0.0 copy-done
  8.6 0.0 copy-done.1
  8.6 0.0 copy-done.3
  8.6 0.0 copy-done.2
  8.6 2.2 %shard_map.74 = (f32[1024,256]{1,0:T(8,128)S(1)}, f32[1024,256]{1,0:T(8,128)S(1)}) custom-call(s32[1,2]{1,0:T(1,128)S(1)} %copy-done.3, s32[1,2,2,16]{3,2,1,0:T(2,128)S(1)} %bitcast.8, bf16[2,256,4096]{2,1,0:T(8,128)(2,1)S(1)} %get-tuple-element.10.held_ref, bf16[256,256]{1,0:T(8,128)(2,1)S(1)} %copy-done.1, bf16[768,256]{1,0:T(8,128)(2,1)S(1)} %copy-done), custom_call_target="tpu_custom_call" | custom-call | flops 1073741824 | bytes 2621440 | tf_op jit(solution)/shard_map/pallas_call | solution.py:169
  10.8 0.0 collective-permute-done.window_ref
  10.8 2.6 %shard_map.75.early_ref = f32[3,8,128]{2,1,0:T(8,128)S(1)} custom-call(f32[1024,256]{1,0:T(8,128)S(1)} %get-tuple-element.11.near_ref, bf16[8,128,128]{2,1,0:T(8,128)(2,1)S(1)} %collective-permute-done.window_ref, bf16[256,256]{1,0:T(8,128)(2,1)S(1)} %copy-done.1, bf16[768,256]{1,0:T(8,128)(2,1)S(1)} %copy-done), custom_call_target="tpu_custom_call" | custom-call | flops 805306368 | bytes 1310720 | tf_op jit(solution)/shard_map/pallas_call | solution.py:275
  13.4 0.9 %collective-permute-done.1.window_ref = bf16[8,128,128]{2,1,0:T(8,128)(2,1)S(1)} collective-permute-done((bf16[8,128,128]{2,1,0:T(8,128)(2,1)S(1)}, bf16[8,128,128]{2,1,0:T(8,128)(2,1)S(1)}, u32[]{:S(2)}, u32[]{:S(2)}) %collective-permute-start.1) | collective-permute-done | bytes 262176 | tf_op jit(solution)/shard_map/ppermute | solution.py:341
  14.3 0.0 copy-done.4
  14.3 0.0 copy-done.5
  14.3 3.3 %shard_map.76 = f32[128,128]{1,0:T(8,128)S(1)} custom-call(s32[1,2]{1,0:T(1,128)S(1)} %copy-done.5, s32[1,2,16]{2,1,0:T(2,128)S(1)} %copy-done.4, f32[3,8,128]{2,1,0:T(8,128)S(1)} %shard_map.75.early_ref, f32[1024,256]{1,0:T(8,128)S(1)} %get-tuple-element.13.near_ref, bf16[8,128,128]{2,1,0:T(8,128)(2,1)S(1)} %collective-permute-done.1.window_ref, ...), custom_call_target="tpu_custom_call" | custom-call | flops 805306368 | bytes 1310720 | tf_op jit(solution)/shard_map/pallas_call | solution.py:286
  17.6 20.2 %all_to_all.5 = f32[128,1,128]{2,1,0:T(1,128)S(1)} all-to-all(f32[128,1,128]{2,1,0:T(1,128)S(1)} %bitcast.6), channel_id=1, replica_groups=mesh['tiles'=64,'grp'=2] {'tiles','grp'}, dimensions={0} | all-to-all | bytes 131072 | tf_op jit(solution)/shard_map/all_to_all | solution.py:354
  37.8 1.2 %shard_map.77 = f32[2,128]{1,0:T(2,128)} custom-call(f32[128,128]{1,0:T(8,128)S(1)} %bitcast.5), custom_call_target="tpu_custom_call" | custom-call | tf_op jit(solution)/shard_map/pallas_call | solution.py:330
Async XLA Ops:
  0.0 8.6 %copy-start = (bf16[768,256]{1,0:T(8,128)(2,1)S(1)}, bf16[768,256]{1,0:T(8,128)(2,1)}, u32[]{:S(2)}) copy-start(bf16[768,256]{1,0:T(8,128)(2,1)} %constant.5.clone.second_ref) | copy-start | bytes 1179652
  0.0 8.6 %copy-start.1 = (bf16[256,256]{1,0:T(8,128)(2,1)S(1)}, bf16[256,256]{1,0:T(8,128)(2,1)}, u32[]{:S(2)}) copy-start(bf16[256,256]{1,0:T(8,128)(2,1)} %constant.4.clone.first_ref) | copy-start | bytes 393220
  0.0 8.6 %copy-start.3 = (s32[1,2]{1,0:T(1,128)S(1)}, s32[1,2]{1,0:T(1,128)}, u32[]{:S(2)}) copy-start(s32[1,2]{1,0:T(1,128)} %colour_ref.1) | copy-start | bytes 28
  0.0 8.6 %copy-start.2 = (s32[1,2,16,2]{2,3,1,0:T(2,128)S(1)}, s32[1,2,16,2]{2,3,1,0:T(2,128)}, u32[]{:S(2)}) copy-start(s32[1,2,16,2]{2,3,1,0:T(2,128)} %param.9) | copy-start | bytes 772
  2.9 11.5 %copy-start.4 = (s32[1,2,16]{2,1,0:T(2,128)S(1)}, s32[1,2,16]{2,1,0:T(2,128)}, u32[]{:S(2)}) copy-start(s32[1,2,16]{2,1,0:T(2,128)} %ids_ref.1) | copy-start | bytes 388
  2.9 11.4 %copy-start.5 = (s32[1,2]{1,0:T(1,128)S(1)}, s32[1,2]{1,0:T(1,128)}, u32[]{:S(2)}) copy-start(s32[1,2]{1,0:T(1,128)} %live_ref.1) | copy-start | bytes 28
  2.9 7.9 %collective-permute-start = (bf16[8,128,128]{2,1,0:T(8,128)(2,1)S(1)}, bf16[8,128,128]{2,1,0:T(8,128)(2,1)S(1)}, u32[]{:S(2)}, u32[]{:S(2)}) collective-permute-start(bf16[8,128,128]{2,1,0:T(8,128)(2,1)S(1)} %get-tuple-element.12), channel_id=1, source_target_pairs={{0,2},{2,0},{4,6},{6,4},{8,10},{10,8},{12,14},{14,12},{16,18},{18,... | collective-permute-start | bytes 786440 | tf_op jit(solution)/shard_map/ppermute | solution.py:341
  5.0 9.3 %collective-permute-start.1 = (bf16[8,128,128]{2,1,0:T(8,128)(2,1)S(1)}, bf16[8,128,128]{2,1,0:T(8,128)(2,1)S(1)}, u32[]{:S(2)}, u32[]{:S(2)}) collective-permute-start(bf16[8,128,128]{2,1,0:T(8,128)(2,1)S(1)} %get-tuple-element.14), channel_id=1, source_target_pairs={{0,64},{2,66},{4,68},{6,70},{8,72},{10,74},{12,76},{14,78},{16,80}... | collective-permute-start | bytes 786440 | tf_op jit(solution)/shard_map/ppermute | solution.py:341

commit v6 on v4

--- a/solution.py
+++ b/solution.py
@@ -243,7 +243,7 @@
     correlate_group(near_ref, window_ref, first_ref, second_ref, late_ref)
     terms = []
     for i in range(3):
-        terms += [early_ref[i], late_ref[i]]
+        terms += [late_ref[i], early_ref[i]]
     terms.append(jnp.zeros((SIDE - 3 * SLOTS, SIDE), f32))
     flat = jnp.concatenate(terms, axis=0).T
     index = lax.broadcasted_iota(jnp.int32, (SIDE, SIDE), 0)
@@ -342,11 +342,11 @@
     tables = [jnp.asarray(table) for table in fourier_tables()]
     corners = jnp.transpose(patch_offsets, (0, 1, 3, 2))
     held, send_early, send_late = hold(edge_colour, corners, strips)
+    far_late = swap(send_late, BITS[1])
     far_early = swap(send_early, BITS[0])
-    far_late = swap(send_late, BITS[1])
     near_early, near_late = near_spectra(edge_colour, corners, held, *tables)
-    early = correlate_early(near_early, far_early, tables)
-    packed = correlate_late(patch_live, node_ids, early, near_late, far_late, tables)
+    early = correlate_early(near_late, far_late, tables)
+    packed = correlate_late(patch_live, node_ids, early, near_early, far_early, tables)
     packed = packed.reshape(SIDE, 1, SIDE)
     gathered = lax.all_to_all(packed, ("tiles", "grp"), 0, 0, tiled=True)
     return collect(gathered.reshape(SIDE, SIDE))

time: 39.2 us -> 40.7 us (1.038)
  waiting for transfers between devices: 0.93 us -> 2.62 us
    ppermute x2, waiting for transfers between devices: 0.93 us -> 2.62 us  [swap(): return lax.ppermute(x, 'tiles', pairs)]
where the time goes in v6:
time: 40.7 us; the launch traced here: 40.5 us
  blocking collectives  20 us (49%)
  Pallas kernels  12.1 us (30%)
  starting transfers between devices  5.72 us (14%)
  waiting for transfers between devices  2.62 us (6%)
    all_to_all x1, blocking collectives, on_device(): gathered = lax.all_to_all(packed, ('tiles', 'grp'), 0, 0, tiled=True)  20 us
    ppermute x2, starting transfers between devices, swap(): return lax.ppermute(x, 'tiles', pairs)  5.72 us
    pallas_call x1, Pallas kernels, correlate_late(): pl.pallas_call(late_kernel, out_shape=jax.ShapeDtypeStruct((SIDE, SIDE),...  3.3 us
    pallas_call x1, Pallas kernels, hold(): pl.pallas_call(hold_kernel, out_shape=(jax.ShapeDtypeStruct(strips.shape,...  2.84 us
    ppermute x2, waiting for transfers between devices, swap(): return lax.ppermute(x, 'tiles', pairs)  2.62 us
    pallas_call x1, Pallas kernels, correlate_early(): pl.pallas_call(correlate_group, out_shape=jax.ShapeDtypeStruct((3, HALF,...  2.56 us
    pallas_call x1, Pallas kernels, near_spectra(): pl.pallas_call(near_kernel, out_shape=(shape, shape), in_specs=[scalars,...  2.19 us
    pallas_call x1, Pallas kernels, collect(): pl.pallas_call(collect_kernel, out_shape=jax.ShapeDtypeStruct((2, SIDE),...  1.2 us
  transfers between devices with their start and end apart: 2, of which 1 were waited for; matrix products, arithmetic and copies ran while one was open for 0% of the time, Pallas kernels for 12%

profile of v6, /device:TPU:1, one launch (start us, length us, event | category | flops | bytes accessed | tf_op | source)
XLA Modules:
  0.0 40.5 jit_solution(424929747606232482)
XLA Ops:
  0.0 0.0 copy-start
  0.0 0.0 copy-start.1
  0.0 0.0 copy-start.3
  0.0 0.0 copy-start.2
  0.0 2.8 %shard_map.73 = (bf16[2,256,4096]{2,1,0:T(8,128)(2,1)S(1)}, bf16[8,128,128]{2,1,0:T(8,128)(2,1)S(1)}, bf16[8,128,128]{2,1,0:T(8,128)(2,1)S(1)}) custom-call(s32[1,2]{1,0:T(1,128)} %colour_ref.1, s32[1,2,2,16]{3,2,1,0:T(2,128)} %bitcast.7, bf16[2,256,4096]{2,1,0:T(8,128)(2,1)} %strips_ref.1), custom_call_target="tpu_custom_call" | custom-call | flops 1048576 | bytes 4194304 | tf_op jit(solution)/shard_map/pallas_call | solution.py:112
  2.9 0.0 copy-start.4
  2.9 0.0 copy-start.5
  2.9 4.5 %collective-permute-start = (bf16[8,128,128]{2,1,0:T(8,128)(2,1)S(1)}, bf16[8,128,128]{2,1,0:T(8,128)(2,1)S(1)}, u32[]{:S(2)}, u32[]{:S(2)}) collective-permute-start(bf16[8,128,128]{2,1,0:T(8,128)(2,1)S(1)} %get-tuple-element.12), channel_id=1, source_target_pairs={{0,64},{2,66},{4,68},{6,70},{8,72},{10,74},{12,76},{14,78},{16,80}... | collective-permute-start | bytes 786440 | tf_op jit(solution)/shard_map/ppermute | solution.py:338
  7.4 1.2 %collective-permute-start.1 = (bf16[8,128,128]{2,1,0:T(8,128)(2,1)S(1)}, bf16[8,128,128]{2,1,0:T(8,128)(2,1)S(1)}, u32[]{:S(2)}, u32[]{:S(2)}) collective-permute-start(bf16[8,128,128]{2,1,0:T(8,128)(2,1)S(1)} %get-tuple-element.14), channel_id=1, source_target_pairs={{0,2},{2,0},{4,6},{6,4},{8,10},{10,8},{12,14},{14,12},{16,18},{18,... | collective-permute-start | bytes 786440 | tf_op jit(solution)/shard_map/ppermute | solution.py:338
  8.6 0.0 copy-done
  8.6 0.0 copy-done.1
  8.6 0.0 copy-done.3
  8.6 0.0 copy-done.2
  8.6 2.2 %shard_map.74 = (f32[1024,256]{1,0:T(8,128)S(1)}, f32[1024,256]{1,0:T(8,128)S(1)}) custom-call(s32[1,2]{1,0:T(1,128)S(1)} %copy-done.3, s32[1,2,2,16]{3,2,1,0:T(2,128)S(1)} %bitcast.8, bf16[2,256,4096]{2,1,0:T(8,128)(2,1)S(1)} %get-tuple-element.10.held_ref, bf16[256,256]{1,0:T(8,128)(2,1)S(1)} %copy-done.1, bf16[768,256]{1,0:T(8,128)(2,1)S(1)} %copy-done), custom_call_target="tpu_custom_call" | custom-call | flops 1073741824 | bytes 2621440 | tf_op jit(solution)/shard_map/pallas_call | solution.py:169
  10.8 2.6 %collective-permute-done.window_ref = bf16[8,128,128]{2,1,0:T(8,128)(2,1)S(1)} collective-permute-done((bf16[8,128,128]{2,1,0:T(8,128)(2,1)S(1)}, bf16[8,128,128]{2,1,0:T(8,128)(2,1)S(1)}, u32[]{:S(2)}, u32[]{:S(2)}) %collective-permute-start) | collective-permute-done | bytes 262176 | tf_op jit(solution)/shard_map/ppermute | solution.py:338
  13.4 2.6 %shard_map.75.early_ref = f32[3,8,128]{2,1,0:T(8,128)S(1)} custom-call(f32[1024,256]{1,0:T(8,128)S(1)} %get-tuple-element.11.near_ref, bf16[8,128,128]{2,1,0:T(8,128)(2,1)S(1)} %collective-permute-done.window_ref, bf16[256,256]{1,0:T(8,128)(2,1)S(1)} %copy-done.1, bf16[768,256]{1,0:T(8,128)(2,1)S(1)} %copy-done), custom_call_target="tpu_custom_call" | custom-call | flops 805306368 | bytes 1310720 | tf_op jit(solution)/shard_map/pallas_call | solution.py:272
  16.0 0.0 collective-permute-done.1.window_ref
  16.0 0.0 copy-done.4
  16.0 0.0 copy-done.5
  16.0 3.3 %shard_map.76 = f32[128,128]{1,0:T(8,128)S(1)} custom-call(s32[1,2]{1,0:T(1,128)S(1)} %copy-done.5, s32[1,2,16]{2,1,0:T(2,128)S(1)} %copy-done.4, f32[3,8,128]{2,1,0:T(8,128)S(1)} %shard_map.75.early_ref, f32[1024,256]{1,0:T(8,128)S(1)} %get-tuple-element.13.near_ref, bf16[8,128,128]{2,1,0:T(8,128)(2,1)S(1)} %collective-permute-done.1.window_ref, ...), custom_call_target="tpu_custom_call" | custom-call | flops 805306368 | bytes 1310720 | tf_op jit(solution)/shard_map/pallas_call | solution.py:283
  19.3 20.0 %all_to_all.5 = f32[128,1,128]{2,1,0:T(1,128)S(1)} all-to-all(f32[128,1,128]{2,1,0:T(1,128)S(1)} %bitcast.6), channel_id=1, replica_groups=mesh['tiles'=64,'grp'=2] {'tiles','grp'}, dimensions={0} | all-to-all | bytes 131072 | tf_op jit(solution)/shard_map/all_to_all | solution.py:351
  39.3 1.2 %shard_map.77 = f32[2,128]{1,0:T(2,128)} custom-call(f32[128,128]{1,0:T(8,128)S(1)} %bitcast.5), custom_call_target="tpu_custom_call" | custom-call | tf_op jit(solution)/shard_map/pallas_call | solution.py:327
Async XLA Ops:
  0.0 8.6 %copy-start = (bf16[768,256]{1,0:T(8,128)(2,1)S(1)}, bf16[768,256]{1,0:T(8,128)(2,1)}, u32[]{:S(2)}) copy-start(bf16[768,256]{1,0:T(8,128)(2,1)} %constant.5.clone.second_ref) | copy-start | bytes 1179652
  0.0 8.6 %copy-start.1 = (bf16[256,256]{1,0:T(8,128)(2,1)S(1)}, bf16[256,256]{1,0:T(8,128)(2,1)}, u32[]{:S(2)}) copy-start(bf16[256,256]{1,0:T(8,128)(2,1)} %constant.4.clone.first_ref) | copy-start | bytes 393220
  0.0 8.6 %copy-start.3 = (s32[1,2]{1,0:T(1,128)S(1)}, s32[1,2]{1,0:T(1,128)}, u32[]{:S(2)}) copy-start(s32[1,2]{1,0:T(1,128)} %colour_ref.1) | copy-start | bytes 28
  0.0 8.6 %copy-start.2 = (s32[1,2,16,2]{2,3,1,0:T(2,128)S(1)}, s32[1,2,16,2]{2,3,1,0:T(2,128)}, u32[]{:S(2)}) copy-start(s32[1,2,16,2]{2,3,1,0:T(2,128)} %param.9) | copy-start | bytes 772
  2.9 13.1 %copy-start.4 = (s32[1,2,16]{2,1,0:T(2,128)S(1)}, s32[1,2,16]{2,1,0:T(2,128)}, u32[]{:S(2)}) copy-start(s32[1,2,16]{2,1,0:T(2,128)} %ids_ref.1) | copy-start | bytes 388
  2.9 13.1 %copy-start.5 = (s32[1,2]{1,0:T(1,128)S(1)}, s32[1,2]{1,0:T(1,128)}, u32[]{:S(2)}) copy-start(s32[1,2]{1,0:T(1,128)} %live_ref.1) | copy-start | bytes 28
  2.9 10.5 %collective-permute-start = (bf16[8,128,128]{2,1,0:T(8,128)(2,1)S(1)}, bf16[8,128,128]{2,1,0:T(8,128)(2,1)S(1)}, u32[]{:S(2)}, u32[]{:S(2)}) collective-permute-start(bf16[8,128,128]{2,1,0:T(8,128)(2,1)S(1)} %get-tuple-element.12), channel_id=1, source_target_pairs={{0,64},{2,66},{4,68},{6,70},{8,72},{10,74},{12,76},{14,78},{16,80}... | collective-permute-start | bytes 786440 | tf_op jit(solution)/shard_map/ppermute | solution.py:338
  7.4 8.6 %collective-permute-start.1 = (bf16[8,128,128]{2,1,0:T(8,128)(2,1)S(1)}, bf16[8,128,128]{2,1,0:T(8,128)(2,1)S(1)}, u32[]{:S(2)}, u32[]{:S(2)}) collective-permute-start(bf16[8,128,128]{2,1,0:T(8,128)(2,1)S(1)} %get-tuple-element.14), channel_id=1, source_target_pairs={{0,2},{2,0},{4,6},{6,4},{8,10},{10,8},{12,14},{14,12},{16,18},{18,... | collective-permute-start | bytes 786440 | tf_op jit(solution)/shard_map/ppermute | solution.py:338

commit v7 on v4

--- a/solution.py
+++ b/solution.py
@@ -59,10 +59,10 @@
         halves = []
         for b in (block, jnp.minimum(block + 1, last)):
             at = pl.ds(pl.multiple_of(b * SIDE, SIDE), SIDE)
-            top = held_ref[colour, :SIDE, at].astype(f32)
-            bottom = held_ref[colour, SIDE:, at].astype(f32)
+            top = held_ref[colour, :SIDE, at]
+            bottom = held_ref[colour, SIDE:, at]
             halves.append(jnp.where(rows >= row, top, bottom))
-        yield jnp.where(lanes >= shift, *halves).astype(bf16)
+        yield jnp.where(lanes >= shift, *halves)
 
 
 def hold_kernel(

time: 39.2 us -> 39.2 us (level)
  no operation moved by 1% of the time
where the time goes in v7:
time: 39.2 us; the launch traced here: 39 us
  blocking collectives  20.2 us (52%)
  Pallas kernels  12.2 us (31%)
  starting transfers between devices  5.72 us (15%)
  waiting for transfers between devices  0.86 us (2%)
    all_to_all x1, blocking collectives, on_device(): gathered = lax.all_to_all(packed, ('tiles', 'grp'), 0, 0, tiled=True)  20.2 us
    ppermute x2, starting transfers between devices, swap(): return lax.ppermute(x, 'tiles', pairs)  5.72 us
    pallas_call x1, Pallas kernels, correlate_late(): pl.pallas_call(late_kernel, out_shape=jax.ShapeDtypeStruct((SIDE, SIDE),...  3.3 us
    pallas_call x1, Pallas kernels, hold(): pl.pallas_call(hold_kernel, out_shape=(jax.ShapeDtypeStruct(strips.shape,...  2.84 us
    pallas_call x1, Pallas kernels, correlate_early(): pl.pallas_call(correlate_group, out_shape=jax.ShapeDtypeStruct((3, HALF,...  2.57 us
    pallas_call x1, Pallas kernels, near_spectra(): pl.pallas_call(near_kernel, out_shape=(shape, shape), in_specs=[scalars,...  2.25 us
    pallas_call x1, Pallas kernels, collect(): pl.pallas_call(collect_kernel, out_shape=jax.ShapeDtypeStruct((2, SIDE),...  1.2 us
    ppermute x2, waiting for transfers between devices, swap(): return lax.ppermute(x, 'tiles', pairs)  0.86 us
  transfers between devices with their start and end apart: 2, of which 1 were waited for; matrix products, arithmetic and copies ran while one was open for 0% of the time, Pallas kernels for 12%

profile of v7, /device:TPU:1, one launch (start us, length us, event | category | flops | bytes accessed | tf_op | source)
XLA Modules:
  0.0 39.0 jit_solution(15789709446582366114)
XLA Ops:
  0.0 0.0 copy-start
  0.0 0.0 copy-start.1
  0.0 0.0 copy-start.3
  0.0 0.0 copy-start.2
  0.0 2.8 %shard_map.73 = (bf16[2,256,4096]{2,1,0:T(8,128)(2,1)S(1)}, bf16[8,128,128]{2,1,0:T(8,128)(2,1)S(1)}, bf16[8,128,128]{2,1,0:T(8,128)(2,1)S(1)}) custom-call(s32[1,2]{1,0:T(1,128)} %colour_ref.1, s32[1,2,2,16]{3,2,1,0:T(2,128)} %bitcast.7, bf16[2,256,4096]{2,1,0:T(8,128)(2,1)} %strips_ref.1), custom_call_target="tpu_custom_call" | custom-call | flops 1048576 | bytes 4194304 | tf_op jit(solution)/shard_map/pallas_call | solution.py:112
  2.9 0.0 copy-start.4
  2.9 0.0 copy-start.5
  2.9 2.1 %collective-permute-start = (bf16[8,128,128]{2,1,0:T(8,128)(2,1)S(1)}, bf16[8,128,128]{2,1,0:T(8,128)(2,1)S(1)}, u32[]{:S(2)}, u32[]{:S(2)}) collective-permute-start(bf16[8,128,128]{2,1,0:T(8,128)(2,1)S(1)} %get-tuple-element.12), channel_id=1, source_target_pairs={{0,2},{2,0},{4,6},{6,4},{8,10},{10,8},{12,14},{14,12},{16,18},{18,... | collective-permute-start | bytes 786440 | tf_op jit(solution)/shard_map/ppermute | solution.py:338
  5.0 3.6 %collective-permute-start.1 = (bf16[8,128,128]{2,1,0:T(8,128)(2,1)S(1)}, bf16[8,128,128]{2,1,0:T(8,128)(2,1)S(1)}, u32[]{:S(2)}, u32[]{:S(2)}) collective-permute-start(bf16[8,128,128]{2,1,0:T(8,128)(2,1)S(1)} %get-tuple-element.14), channel_id=1, source_target_pairs={{0,64},{2,66},{4,68},{6,70},{8,72},{10,74},{12,76},{14,78},{16,80}... | collective-permute-start | bytes 786440 | tf_op jit(solution)/shard_map/ppermute | solution.py:338
  8.6 0.0 copy-done
  8.6 0.0 copy-done.1
  8.6 0.0 copy-done.3
  8.6 0.0 copy-done.2
  8.6 2.2 %shard_map.74 = (f32[1024,256]{1,0:T(8,128)S(1)}, f32[1024,256]{1,0:T(8,128)S(1)}) custom-call(s32[1,2]{1,0:T(1,128)S(1)} %copy-done.3, s32[1,2,2,16]{3,2,1,0:T(2,128)S(1)} %bitcast.8, bf16[2,256,4096]{2,1,0:T(8,128)(2,1)S(1)} %get-tuple-element.10.held_ref, bf16[256,256]{1,0:T(8,128)(2,1)S(1)} %copy-done.1, bf16[768,256]{1,0:T(8,128)(2,1)S(1)} %copy-done), custom_call_target="tpu_custom_call" | custom-call | flops 1073741824 | bytes 2621440 | tf_op jit(solution)/shard_map/pallas_call | solution.py:169
  10.9 0.0 collective-permute-done.window_ref
  10.9 2.6 %shard_map.75.early_ref = f32[3,8,128]{2,1,0:T(8,128)S(1)} custom-call(f32[1024,256]{1,0:T(8,128)S(1)} %get-tuple-element.11.near_ref, bf16[8,128,128]{2,1,0:T(8,128)(2,1)S(1)} %collective-permute-done.window_ref, bf16[256,256]{1,0:T(8,128)(2,1)S(1)} %copy-done.1, bf16[768,256]{1,0:T(8,128)(2,1)S(1)} %copy-done), custom_call_target="tpu_custom_call" | custom-call | flops 805306368 | bytes 1310720 | tf_op jit(solution)/shard_map/pallas_call | solution.py:272
  13.5 0.9 %collective-permute-done.1.window_ref = bf16[8,128,128]{2,1,0:T(8,128)(2,1)S(1)} collective-permute-done((bf16[8,128,128]{2,1,0:T(8,128)(2,1)S(1)}, bf16[8,128,128]{2,1,0:T(8,128)(2,1)S(1)}, u32[]{:S(2)}, u32[]{:S(2)}) %collective-permute-start.1) | collective-permute-done | bytes 262176 | tf_op jit(solution)/shard_map/ppermute | solution.py:338
  14.3 0.0 copy-done.4
  14.3 0.0 copy-done.5
  14.3 3.3 %shard_map.76 = f32[128,128]{1,0:T(8,128)S(1)} custom-call(s32[1,2]{1,0:T(1,128)S(1)} %copy-done.5, s32[1,2,16]{2,1,0:T(2,128)S(1)} %copy-done.4, f32[3,8,128]{2,1,0:T(8,128)S(1)} %shard_map.75.early_ref, f32[1024,256]{1,0:T(8,128)S(1)} %get-tuple-element.13.near_ref, bf16[8,128,128]{2,1,0:T(8,128)(2,1)S(1)} %collective-permute-done.1.window_ref, ...), custom_call_target="tpu_custom_call" | custom-call | flops 805306368 | bytes 1310720 | tf_op jit(solution)/shard_map/pallas_call | solution.py:283
  17.6 20.2 %all_to_all.5 = f32[128,1,128]{2,1,0:T(1,128)S(1)} all-to-all(f32[128,1,128]{2,1,0:T(1,128)S(1)} %bitcast.6), channel_id=1, replica_groups=mesh['tiles'=64,'grp'=2] {'tiles','grp'}, dimensions={0} | all-to-all | bytes 131072 | tf_op jit(solution)/shard_map/all_to_all | solution.py:351
  37.8 1.2 %shard_map.77 = f32[2,128]{1,0:T(2,128)} custom-call(f32[128,128]{1,0:T(8,128)S(1)} %bitcast.5), custom_call_target="tpu_custom_call" | custom-call | tf_op jit(solution)/shard_map/pallas_call | solution.py:327
Async XLA Ops:
  0.0 8.6 %copy-start = (bf16[768,256]{1,0:T(8,128)(2,1)S(1)}, bf16[768,256]{1,0:T(8,128)(2,1)}, u32[]{:S(2)}) copy-start(bf16[768,256]{1,0:T(8,128)(2,1)} %constant.5.clone.second_ref) | copy-start | bytes 1179652
  0.0 8.6 %copy-start.1 = (bf16[256,256]{1,0:T(8,128)(2,1)S(1)}, bf16[256,256]{1,0:T(8,128)(2,1)}, u32[]{:S(2)}) copy-start(bf16[256,256]{1,0:T(8,128)(2,1)} %constant.4.clone.first_ref) | copy-start | bytes 393220
  0.0 8.6 %copy-start.3 = (s32[1,2]{1,0:T(1,128)S(1)}, s32[1,2]{1,0:T(1,128)}, u32[]{:S(2)}) copy-start(s32[1,2]{1,0:T(1,128)} %colour_ref.1) | copy-start | bytes 28
  0.0 8.6 %copy-start.2 = (s32[1,2,16,2]{2,3,1,0:T(2,128)S(1)}, s32[1,2,16,2]{2,3,1,0:T(2,128)}, u32[]{:S(2)}) copy-start(s32[1,2,16,2]{2,3,1,0:T(2,128)} %param.9) | copy-start | bytes 772
  2.9 11.5 %copy-start.4 = (s32[1,2,16]{2,1,0:T(2,128)S(1)}, s32[1,2,16]{2,1,0:T(2,128)}, u32[]{:S(2)}) copy-start(s32[1,2,16]{2,1,0:T(2,128)} %ids_ref.1) | copy-start | bytes 388
  2.9 11.4 %copy-start.5 = (s32[1,2]{1,0:T(1,128)S(1)}, s32[1,2]{1,0:T(1,128)}, u32[]{:S(2)}) copy-start(s32[1,2]{1,0:T(1,128)} %live_ref.1) | copy-start | bytes 28
  2.9 8.0 %collective-permute-start = (bf16[8,128,128]{2,1,0:T(8,128)(2,1)S(1)}, bf16[8,128,128]{2,1,0:T(8,128)(2,1)S(1)}, u32[]{:S(2)}, u32[]{:S(2)}) collective-permute-start(bf16[8,128,128]{2,1,0:T(8,128)(2,1)S(1)} %get-tuple-element.12), channel_id=1, source_target_pairs={{0,2},{2,0},{4,6},{6,4},{8,10},{10,8},{12,14},{14,12},{16,18},{18,... | collective-permute-start | bytes 786440 | tf_op jit(solution)/shard_map/ppermute | solution.py:338
  5.0 9.3 %collective-permute-start.1 = (bf16[8,128,128]{2,1,0:T(8,128)(2,1)S(1)}, bf16[8,128,128]{2,1,0:T(8,128)(2,1)S(1)}, u32[]{:S(2)}, u32[]{:S(2)}) collective-permute-start(bf16[8,128,128]{2,1,0:T(8,128)(2,1)S(1)} %get-tuple-element.14), channel_id=1, source_target_pairs={{0,64},{2,66},{4,68},{6,70},{8,72},{10,74},{12,76},{14,78},{16,80}... | collective-permute-start | bytes 786440 | tf_op jit(solution)/shard_map/ppermute | solution.py:338
